TPU v7x, 128 devices: a whole 4x4x4 slice. The times are simulated.
128 devices in a mesh: row: 4 (over y), col: 4 (over x_hi, core), en: 8 (over x_lo, z).
Axes of the slice: x: 4 (x_hi: 2, x_lo: 2; x = x_hi * 2 + x_lo), y: 4, z: 4, core: 2. Of those that a mesh axis runs over, the one named last changes fastest.
Arguments:
- lesser: bfloat16 [2, 4, 3, 128, 512, 128], P(None, 'row', None, 'col', 'en'), may hold values from -6 to 6
- greater: bfloat16 [2, 4, 3, 128, 512, 128], P(None, 'row', None, 'col', 'en'), may hold values from -6 to 6
- coupling: bfloat16 [4, 3, 128, 128], replicated, may hold values from -0.3125 to 0.3125
Outputs:
- screened: bfloat16 [2, 4, 5, 128, 512, 128], P(None, 'row', None, None, ('col', 'en'))
All inputs are finite; a program needn't handle non-finite values.
Results may differ from a plain program's by a relative error of at most 0.025.
Values may be sent and summed in bfloat16 or wider, within the bound.
A program may use at most 128 MiB of HBM per device.

v0:
```python
import math

import jax
import jax.numpy as jnp
from jax import lax
from jax.sharding import PartitionSpec as P


def extended(cells, sides, width):
    for axis, dim in sides:
        count = lax.axis_size(axis)
        ends = count - 1
        head = lax.slice_in_dim(cells, 0, width, axis=dim)
        tail = lax.slice_in_dim(cells, cells.shape[dim] - width, cells.shape[dim], axis=dim)
        cells = jnp.concatenate(
            [
                lax.ppermute(tail, axis, [(i, (i + 1) % count) for i in range(ends)]),
                cells,
                lax.ppermute(head, axis, [((i + 1) % count, i) for i in range(ends)]),
            ],
            axis=dim,
        )
    return cells


def keep_rounded(values):
    return lax.optimization_barrier(values.astype(jnp.bfloat16)).astype(jnp.float32)


def forward_table(length, count):
    freq_index = jnp.arange(length, dtype=jnp.int32)
    energy_index = jnp.arange(count, dtype=jnp.int32)
    phases = energy_index[:, None] * freq_index[None, :] % length
    angles = phases.astype(jnp.float32) * (2.0 * math.pi / length)
    return jnp.stack([jnp.cos(angles), jnp.sin(angles)], axis=1).astype(jnp.bfloat16)


def inverse_table(length, count):
    freq_index = jnp.arange(length, dtype=jnp.int32)
    lag_index = (jnp.arange(count, dtype=jnp.int32) - count // 2 + length) % length
    phases = freq_index[:, None] * lag_index[None, :] % length
    angles = phases.astype(jnp.float32) * (2.0 * math.pi / length)
    stacked = jnp.stack([jnp.cos(angles), jnp.sin(angles)], axis=1) / length
    return stacked.astype(jnp.bfloat16)


def split_parts(spectrum, sign):
    real_part = spectrum[0, 0] + sign * spectrum[1, 1]
    imag_part = spectrum[1, 0] - sign * spectrum[0, 1]
    return (
        real_part.astype(jnp.bfloat16).astype(jnp.float32),
        imag_part.astype(jnp.bfloat16).astype(jnp.float32),
    )


def shards(lesser, greater, coupling):
    tile_rows = lesser.shape[1]
    row_part = lesser.shape[3]
    energy_part = lesser.shape[4]
    orbitals = lesser.shape[5]
    col_count = lax.axis_size("col")
    energy_count = lax.axis_size("en")
    row_count = lax.axis_size("row")
    energies = energy_part * energy_count
    length = 2 * energies
    pieces = row_part // energy_count
    first_row = lax.axis_index("row") * tile_rows
    total_rows = tile_rows * row_count
    edges = jnp.concatenate([greater[:, :1, 0], greater[:, -1:, 2]], axis=1)
    rims = extended(edges, (("row", 1),), 1)
    from_below = jnp.concatenate([rims[:, :1], greater[:, :-1, 2]], axis=1)
    from_above = jnp.concatenate([greater[:, 1:, 0], rims[:, 3:]], axis=1)
    mirror = jnp.stack([from_below, greater[:, :, 1], from_above], axis=2)
    spread = lesser.reshape(2, tile_rows, 3, energy_count, pieces, energy_part, orbitals)
    spread = lax.all_to_all(spread, "en", split_axis=3, concat_axis=5, tiled=True)
    spread = spread.reshape(2, tile_rows, 3, pieces, energies, orbitals)
    forward = forward_table(length, energies)
    parcel = mirror.reshape(
        2, tile_rows, 3, 1, row_part, energy_part, col_count * energy_count, pieces
    )
    moved = lax.all_to_all(parcel, ("col", "en"), split_axis=6, concat_axis=3, tiled=True)
    moved = moved.reshape(2, tile_rows, 3, col_count, energy_count, row_part, energy_part, pieces)
    split_table = forward.reshape(energy_count, energy_part, 2, length)
    inverse = inverse_table(length, energies)
    scale = 1.0 / math.sqrt(length)
    row_numbers = first_row + jnp.arange(tile_rows, dtype=jnp.int32)
    polar = []
    for slot in range(3):
        first_raw = jnp.einsum(
            "xkamb,myf->xykabf", spread[:, :, slot], forward, preferred_element_type=jnp.float32
        )
        one_re, one_im = split_parts(first_raw, 1.0)
        second_result = jnp.einsum(
            "xkcebma,emyf->xykacbf",
            moved[:, :, slot],
            split_table,
            preferred_element_type=jnp.float32,
        )
        two_re, two_im = split_parts(
            second_result.reshape(2, 2, tile_rows, pieces, orbitals, length), -1.0
        )
        product = jnp.stack(
            [one_re * two_re - one_im * two_im, one_re * two_im + one_im * two_re]
        ).astype(jnp.bfloat16)
        lagged = jnp.einsum(
            "xkabf,fyl->xykalb", product, inverse, preferred_element_type=jnp.float32
        )
        lag_re = lagged[0, 0] - lagged[1, 1]
        lag_im = lagged[0, 1] + lagged[1, 0]
        partner = row_numbers + slot - 1
        inside = ((partner >= 0) & (partner < total_rows)).astype(jnp.float32)[
            None, :, None, None, None
        ]
        polar.append((jnp.stack([scale * lag_im, -scale * lag_re]) * inside).astype(jnp.bfloat16))
    padded = jnp.pad(coupling, ((2, 2), (0, 0), (0, 0), (0, 0)))
    window = lax.dynamic_slice_in_dim(padded, first_row, tile_rows + 4, 0)
    halves = []
    for band in range(5):
        total = jnp.zeros((2, tile_rows, pieces, energies, orbitals), jnp.float32)
        for slot in range(3):
            offset = band - slot
            if 0 <= offset <= 2:
                tiles = window[band : band + tile_rows, 2 - offset]
                term = jnp.einsum(
                    "xkaln,kmn->xkalm", polar[slot], tiles, preferred_element_type=jnp.float32
                )
                total = total + keep_rounded(term)
        halves.append(total.astype(jnp.bfloat16))
    half = jnp.stack(halves, axis=2)
    gathered = lax.all_to_all(half, ("col", "en"), split_axis=4, concat_axis=3, tiled=True)
    borders = jnp.concatenate([gathered[:, :1, 0:4], gathered[:, -1:, 1:5]], axis=1)
    outer = extended(borders, (("row", 1),), 1)
    lower = jnp.concatenate([outer[:, :1], gathered[:, :-1, 1:5]], axis=1)
    upper = jnp.concatenate([gathered[:, 1:, 0:4], outer[:, 3:]], axis=1)
    local_tiles = lax.dynamic_slice_in_dim(coupling, first_row, tile_rows, 0)
    middle = keep_rounded(
        jnp.einsum(
            "kmj,xksjln->xksmln", local_tiles[:, 1], gathered, preferred_element_type=jnp.float32
        )
    )
    below_term = keep_rounded(
        jnp.einsum(
            "kmj,xksjln->xksmln", local_tiles[:, 0], lower, preferred_element_type=jnp.float32
        )
    )
    above_term = keep_rounded(
        jnp.einsum(
            "kmj,xksjln->xksmln", local_tiles[:, 2], upper, preferred_element_type=jnp.float32
        )
    )
    blank = jnp.zeros_like(middle[:, :, :1])
    result = (
        middle
        + jnp.concatenate([below_term, blank], axis=2)
        + jnp.concatenate([blank, above_term], axis=2)
    )
    return result.astype(jnp.bfloat16)


def solution(mesh):
    placed = (P(None, "row", None, "col", "en", None), P(None, "row", None, "col", "en", None), P())
    return jax.shard_map(
        shards,
        mesh=mesh,
        in_specs=placed,
        out_specs=P(None, "row", None, None, ("col", "en"), None),
        check_vma=False,
    )
```

profile of v0, /device:TPU:24, one launch (start us, length us, event | category | flops | bytes accessed | tf_op | source)
XLA Modules:
  0.0 477.8 jit_solution(15074759937619373507)
XLA Ops:
  0.0 4.7 copy.120
  4.7 6.2 %all-to-all-start = ((bf16[2,1,3,8,4,64,128]{6,5,4,0,2,1,3:T(8,128)(2,1)}), bf16[2,1,3,8,4,64,128]{6,5,4,0,2,1,3:T(8,128)(2,1)S(1)}, u32[]{:S(2)}, u32[]{:S(2)}) async-start(bf16[2,1,3,8,4,64,128]{6,5,4,0,2,1,3:T(8,128)(2,1)} %copy.120), calls=%async_computation | async-start | bytes 6291456 | tf_op jit(solution)/shard_map/all_to_all | solution.py:75
  11.0 3.7 slice_bitcast_fusion.11
  15.9 5.5 %collective-permute-start.1 = (bf16[2,1,32,64,128]{4,3,2,1,0:T(8,128)(2,1)}, bf16[2,1,32,64,128]{4,3,2,1,0:T(8,128)(2,1)}, u32[]{:S(2)}, u32[]{:S(2)}) collective-permute-start(bf16[2,1,32,64,128]{4,3,2,1,0:T(8,128)(2,1)} %get-tuple-element.43), channel_id=1, source_target_pairs={{32,0},{64,32},{96,64},{33,1},{65,33},{97,65},{34,2},{66,34},{98,6... | collective-permute-start | bytes 3145736 | tf_op jit(solution)/shard_map/ppermute | solution.py:19
  21.5 4.7 copy.207
  26.1 15.3 %collective-permute-done = bf16[2,1,32,64,128]{4,3,2,1,0:T(8,128)(2,1)} collective-permute-done((bf16[2,1,32,64,128]{4,3,2,1,0:T(8,128)(2,1)}, bf16[2,1,32,64,128]{4,3,2,1,0:T(8,128)(2,1)}, u32[]{:S(2)}, u32[]{:S(2)}) %collective-permute-start) | collective-permute-done | bytes 1048608 | tf_op jit(solution)/shard_map/ppermute | solution.py:17
  41.5 4.7 copy.125
  46.1 4.6 copy.128
  50.8 7.5 %copy_bitcast_fusion.6 = bf16[32,1,3,1,2,4,32,64]{7,6,5,4,3,2,1,0:T(8,128)(2,1)} fusion(bf16[2,1,1,1,32,64,32,4]{5,4,7,6,0,3,2,1:T(8,128)(2,1)} %bitcast.397, bf16[2,1,1,1,32,64,32,4]{5,4,7,6,0,3,2,1:T(8,128)(2,1)} %bitcast.395, bf16[2,1,1,1,32,64,32,4]{5,4,7,6,0,3,2,1:T(8,128)(2,1)} %bitcast.396), kind=kLoop, calls=%fused_computation.249 | loop fusion | flops 3145728 | bytes 6291456
  58.2 8.7 %reshape.1443 = bf16[32,2,24576]{2,1,0:T(2,128)(2,1)} reshape(bf16[32,1,3,1,2,4,32,64]{7,6,5,4,3,2,1,0:T(8,128)(2,1)} %copy_bitcast_fusion.6) | data formatting | bytes 6291456
  67.0 7.4 %all-to-all-start.1 = ((bf16[32,2,24576]{2,1,0:T(2,128)(2,1)}), bf16[32,2,24576]{2,1,0:T(2,128)(2,1)}, u32[]{:S(2)}, u32[]{:S(2)}) async-start(bf16[32,2,24576]{2,1,0:T(2,128)(2,1)} %reshape.1443), calls=%async_computation.1 | async-start | bytes 6291456 | tf_op jit(solution)/shard_map/all_to_all | solution.py:81
  74.4 8.5 %sine_convert_fusion.1 = (bf16[512,1,1024]{0,2,1:T(8,128)(2,1)S(1)}, bf16[512,1,1024]{0,2,1:T(8,128)(2,1)S(1)}) fusion(), kind=kLoop, calls=%fused_computation.120 | loop fusion | flops 8388608 | bytes 2097152 | tf_op jit(solution)/shard_map/convert.25
  82.9 10.6 %fusion.101 = (f32[1024,1,512]{0,2,1:T(8,128)}, f32[1024,1,512]{0,2,1:T(8,128)}) fusion(s32[512]{0:T(512)S(1)} %add_select_fusion.3), kind=kLoop, calls=%fused_computation.196 | loop fusion | flops 7340032 | bytes 4196352 | tf_op jit(solution)/shard_map/cos | solution.py:43
  93.5 10.6 %cosine_convert_fusion = (bf16[8,64,1,1024]{3,1,0,2:T(8,128)(2,1)}, bf16[8,64,1,1024]{3,1,0,2:T(8,128)(2,1)}) fusion(s32[8,64]{1,0:T(8,128)S(1)} %multiply_add_fusion), kind=kLoop, calls=%fused_computation.117 | loop fusion | flops 8388608 | bytes 2099200 | tf_op jit(solution)/shard_map/convert.22
  105.0 5.6 %convolution_bitcast_fusion.1 = f32[2,2,1,4,128,1024]{4,5,3,2,1,0:T(8,128)} fusion(bf16[2,1,3,4,512,128]{5,4,3,0,2,1:T(8,128)(2,1)S(1)} %bitcast.399, bf16[512,1,1024]{0,2,1:T(8,128)(2,1)S(1)} %get-tuple-element.48, bf16[512,1,1024]{0,2,1:T(8,128)(2,1)S(1)} %get-tuple-element.49), kind=kOutput, calls=%fused_computation.14 | convolution fusion | flops 2151677952 | bytes 11534336 | tf_op jit(solution)/shard_map/xkamb,myf->xykabf/dot_general | solution.py:89
  110.6 5.6 %convolution_bitcast_fusion.3 = f32[2,2,1,4,128,1024]{4,5,3,2,1,0:T(8,128)} fusion(bf16[2,1,3,4,512,128]{5,4,3,0,2,1:T(8,128)(2,1)S(1)} %bitcast.400, bf16[512,1,1024]{0,2,1:T(8,128)(2,1)S(1)} %get-tuple-element.48, bf16[512,1,1024]{0,2,1:T(8,128)(2,1)S(1)} %get-tuple-element.49), kind=kOutput, calls=%fused_computation.16 | convolution fusion | flops 2151677952 | bytes 11534336 | tf_op jit(solution)/shard_map/xkamb,myf->xykabf/dot_general | solution.py:89
  116.3 5.7 %convolution_bitcast_fusion.5 = f32[2,2,1,4,128,1024]{4,5,3,0,1,2:T(8,128)} fusion(bf16[2,1,3,4,512,128]{5,4,3,0,2,1:T(8,128)(2,1)S(1)} %bitcast.401, bf16[512,1,1024]{0,2,1:T(8,128)(2,1)S(1)} %get-tuple-element.48, bf16[512,1,1024]{0,2,1:T(8,128)(2,1)S(1)} %get-tuple-element.49), kind=kOutput, calls=%fused_computation.18 | convolution fusion | flops 2151677952 | bytes 11534336 | tf_op jit(solution)/shard_map/xkamb,myf->xykabf/dot_general | solution.py:89
  121.9 9.0 %reshape.1444 = bf16[32,1,3,1,2,4,32,64]{7,6,5,4,3,2,1,0:T(8,128)(2,1)} reshape(bf16[32,2,24576]{2,1,0:T(2,128)(2,1)} %all-to-all-done.1) | data formatting | bytes 6291456
  130.9 4.4 copy.130
  135.3 3.6 fusion.154
  138.8 2.5 convolution_bitcast_fusion.4
  141.3 1.7 copy.132
  143.0 3.5 fusion.153
  146.4 1.9 copy.210
  148.3 2.9 copy.211
  151.2 2.9 copy.212
  154.2 3.4 copy.213
  157.5 6.4 %fusion.85 = (bf16[1,4,128,1024]{2,3,1,0:T(8,128)(2,1)S(1)}, bf16[1,1,1,4,128,1024]{4,5,3,2,1,0:T(8,128)(2,1)S(1)}, bf16[1,1,1,4,128,1024]{4,5,3,2,1,0:T(8,128)(...) fusion(f32[2,2,1,4,128,1024]{4,5,3,0,1,2:T(8,128)} %convolution_bitcast_fusion.5, ...), kind=kLoop, calls=%fused_computation.166 | loop fusion | flops 9437184 | bytes 22020096 | tf_op jit(solution)/shard_map/convert.20
  166.1 2.3 convolution_bitcast_fusion.8
  171.1 2.5 convolution_bitcast_fusion.2
  173.5 1.7 copy.146
  175.2 3.4 fusion.152
  178.6 1.9 copy.217
  180.5 2.9 copy.218
  183.4 2.9 copy.219
  186.4 3.1 copy.220
  189.4 7.3 %fusion.84 = (bf16[1,4,128,1024]{2,3,1,0:T(8,128)(2,1)}, bf16[1,1,1,4,128,1024]{4,5,3,2,1,0:T(8,128)(2,1)S(1)}, bf16[1,1,1,4,128,1024]{4,5,3,2,1,0:T(8,128)(2,1)...) fusion(f32[2,2,1,4,128,1024]{4,5,3,2,1,0:T(8,128)} %convolution_bitcast_fusion.3, ...), kind=kLoop, calls=%fused_computation.165 | loop fusion | flops 9437184 | bytes 22020096 | tf_op jit(solution)/shard_map/convert.18
  199.2 2.3 convolution_bitcast_fusion.7
  204.0 1.5 fusion.66
  211.2 2.5 convolution_bitcast_fusion
  213.6 1.7 copy.155
  215.3 3.5 fusion.151
  218.8 1.9 copy.222
  220.7 2.9 copy.223
  223.6 2.9 copy.224
  226.5 3.1 copy.225
  229.5 7.3 %fusion.82 = (bf16[1,4,128,1024]{2,3,1,0:T(8,128)(2,1)}, bf16[1,1,1,4,128,1024]{4,5,3,2,1,0:T(8,128)(2,1)S(1)}, bf16[1,1,1,4,128,1024]{4,5,3,2,1,0:T(8,128)(2,1)...) fusion(f32[2,2,1,4,128,1024]{4,5,3,2,1,0:T(8,128)} %convolution_bitcast_fusion.1, ...), kind=kLoop, calls=%fused_computation.163 | loop fusion | flops 9437184 | bytes 22020096 | tf_op jit(solution)/shard_map/convert.16
  239.3 2.3 convolution_bitcast_fusion.6
  247.6 1.5 fusion.78
  251.4 9.2 %copy.162 = bf16[2,1,5,4,512,128]{5,3,0,2,1,4:T(4,128)(2,1)} copy(bf16[2,1,5,4,512,128]{4,5,3,0,2,1:T(8,128)(2,1)} %bitcast_dynamic-update-slice_fusion) | data formatting | bytes 10485760 | tf_op jit(solution)/shard_map/stack | solution.py:129
  260.6 68.7 %all_to_all.48 = bf16[2,1,5,4,512,128]{5,3,0,2,1,4:T(4,128)(2,1)S(1)} all-to-all(bf16[2,1,5,4,512,128]{5,3,0,2,1,4:T(4,128)(2,1)} %copy.162), channel_id=1, replica_groups=mesh['row'=4,'col'=4,'en'=8] {'col','en'}, dimensions={4} | all-to-all | bytes 10485760 | tf_op jit(solution)/shard_map/all_to_all | solution.py:130
  330.5 1.5 copy.164
  332.0 4.4 fusion.155
  336.9 7.9 %copy.227 = bf16[2,1,4,128,16,128]{3,5,4,2,0,1:T(8,128)(2,1)} copy(bf16[2,1,4,128,16,128]{5,4,3,2,0,1:T(8,128)(2,1)} %get-tuple-element.36) | data formatting | bytes 8388608
  344.7 4.7 collective-permute-start.3
  349.5 7.9 %copy.226 = bf16[2,1,4,128,16,128]{3,5,4,2,0,1:T(8,128)(2,1)} copy(bf16[2,1,4,128,16,128]{5,4,3,2,0,1:T(8,128)(2,1)} %get-tuple-element.35) | data formatting | bytes 8388608
  357.3 1.5 collective-permute-start.2
  358.9 6.5 %convert_bitcast_fusion = bf16[2,1,5,128,16,128]{3,5,4,2,0,1:T(8,128)(2,1)} fusion(bf16[2,5,128,16,128]{4,3,2,1,0:T(8,128)(2,1)} %bitcast.387, bf16[4,3,128,128]{3,2,1,0:T(8,128)(2,1)S(1)} %copy-done.1, s32[]{:T(128)S(6)} %select_n.74, s32[]{:T(128)S(6)} %add.357), kind=kOutput, calls=%fused_computation.4 | convolution fusion | flops 673710080 | bytes 10518536 | tf_op jit(solution)/shard_map/kmj,xksjln->xksmln/dot_general | solution.py:137
  365.3 72.7 %collective-permute-done.3 = bf16[2,1,4,128,16,128]{3,5,4,2,0,1:T(8,128)(2,1)} collective-permute-done((bf16[2,1,4,128,16,128]{3,5,4,2,0,1:T(8,128)(2,1)}, bf16[2,1,4,128,16,128]{3,5,4,2,0,1:T(8,128)(2,1)}, u32[]{:S(2)}, u32[]{:S(2)}) %collective-permute-start.3) | collective-permute-done | bytes 4194336 | tf_op jit(solution)/shard_map/ppermute | solution.py:19
  438.1 5.5 %convert_bitcast_fusion.1 = bf16[2,1,4,128,16,128]{3,5,4,2,0,1:T(8,128)(2,1)} fusion(bf16[2,1,4,128,16,128]{3,5,4,2,0,1:T(8,128)(2,1)} %collective-permute-done.3, bf16[4,3,128,128]{3,2,1,0:T(8,128)(2,1)S(1)} %copy-done.1, s32[]{:T(128)S(6)} %select_n.74, s32[]{:T(128)S(6)} %add.355), kind=kOutput, calls=%fused_computation.11 | convolution fusion | flops 538968064 | bytes 8421384 | tf_op jit(solution)/shard_map/kmj,xksjln->xksmln/dot_general | solution.py:147
  443.5 8.6 %collective-permute-done.2 = bf16[2,1,4,128,16,128]{3,5,4,2,0,1:T(8,128)(2,1)} collective-permute-done((bf16[2,1,4,128,16,128]{3,5,4,2,0,1:T(8,128)(2,1)}, bf16[2,1,4,128,16,128]{3,5,4,2,0,1:T(8,128)(2,1)}, u32[]{:S(2)}, u32[]{:S(2)}) %collective-permute-start.2) | collective-permute-done | bytes 4194336 | tf_op jit(solution)/shard_map/ppermute | solution.py:17
  452.1 5.5 %convert_bitcast_fusion.2 = bf16[2,1,4,128,16,128]{3,5,4,2,0,1:T(8,128)(2,1)} fusion(bf16[2,1,4,128,16,128]{3,5,4,2,0,1:T(8,128)(2,1)} %collective-permute-done.2, bf16[4,3,128,128]{3,2,1,0:T(8,128)(2,1)S(1)} %copy-done.1, s32[]{:T(128)S(6)} %select_n.74), kind=kOutput, calls=%fused_computation.12 | convolution fusion | flops 538968064 | bytes 8421380 | tf_op jit(solution)/shard_map/kmj,xksjln->xksmln/dot_general | solution.py:142
  457.5 11.6 %add_convert_fusion = bf16[2,1,5,128,16,128]{3,5,4,2,0,1:T(8,128)(2,1)} fusion(bf16[2,1,5,128,16,128]{3,5,4,2,0,1:T(8,128)(2,1)} %convert_bitcast_fusion, bf16[2,1,4,128,16,128]{3,5,4,2,0,1:T(8,128)(2,1)} %convert_bitcast_fusion.1, bf16[2,1,4,128,16,128]{3,5,4,2,0,1:T(8,128)(2,1)} %convert_bitcast_fusion.2), kind=kLoop, calls=%fused_computation | loop fusion | flops 15728640 | bytes 18874368 | tf_op jit(solution)/shard_map/convert_element_type | solution.py:157
  469.1 8.2 %copy.169 = bf16[2,1,5,128,16,128]{5,4,3,2,1,0:T(8,128)(2,1)} copy(bf16[2,1,5,128,16,128]{3,5,4,2,0,1:T(8,128)(2,1)} %add_convert_fusion) | data formatting | bytes 10485760 | tf_op jit(solution)/shard_map/convert_element_type | solution.py:157
  (78 shorter events, 29.9 us)
Async XLA Ops:
  4.7 62.2 %all-to-all-start = ((bf16[2,1,3,8,4,64,128]{6,5,4,0,2,1,3:T(8,128)(2,1)}), bf16[2,1,3,8,4,64,128]{6,5,4,0,2,1,3:T(8,128)(2,1)S(1)}, u32[]{:S(2)}, u32[]{:S(2)}) async-start(bf16[2,1,3,8,4,64,128]{6,5,4,0,2,1,3:T(8,128)(2,1)} %copy.120), calls=%async_computation | async-start | bytes 6291456 | tf_op jit(solution)/shard_map/all_to_all | solution.py:75
  14.6 26.8 %collective-permute-start = (bf16[2,1,32,64,128]{4,3,2,1,0:T(8,128)(2,1)}, bf16[2,1,32,64,128]{4,3,2,1,0:T(8,128)(2,1)}, u32[]{:S(2)}, u32[]{:S(2)}) collective-permute-start(bf16[2,1,32,64,128]{4,3,2,1,0:T(8,128)(2,1)} %get-tuple-element.41), channel_id=1, source_target_pairs={{0,32},{32,64},{64,96},{1,33},{33,65},{65,97},{2,34},{34,66},{66,9... | collective-permute-start | bytes 3145736 | tf_op jit(solution)/shard_map/ppermute | solution.py:17
  15.9 30.2 %collective-permute-start.1 = (bf16[2,1,32,64,128]{4,3,2,1,0:T(8,128)(2,1)}, bf16[2,1,32,64,128]{4,3,2,1,0:T(8,128)(2,1)}, u32[]{:S(2)}, u32[]{:S(2)}) collective-permute-start(bf16[2,1,32,64,128]{4,3,2,1,0:T(8,128)(2,1)} %get-tuple-element.43), channel_id=1, source_target_pairs={{32,0},{64,32},{96,64},{33,1},{65,33},{97,65},{34,2},{66,34},{98,6... | collective-permute-start | bytes 3145736 | tf_op jit(solution)/shard_map/ppermute | solution.py:19
  67.0 55.0 %all-to-all-start.1 = ((bf16[32,2,24576]{2,1,0:T(2,128)(2,1)}), bf16[32,2,24576]{2,1,0:T(2,128)(2,1)}, u32[]{:S(2)}, u32[]{:S(2)}) async-start(bf16[32,2,24576]{2,1,0:T(2,128)(2,1)} %reshape.1443), calls=%async_computation.1 | async-start | bytes 6291456 | tf_op jit(solution)/shard_map/all_to_all | solution.py:81
  135.3 3.6 copy-start.16
  135.3 3.6 copy-start.19
  163.9 1.6 copy-start.8
  163.9 2.2 copy-start.11
  168.5 1.3 copy-start.20
  168.6 2.2 copy-start.15
  168.6 2.4 copy-start.17
  196.8 1.6 copy-start.9
  196.8 2.2 copy-start.12
  196.8 2.5 copy-start.23
  201.8 1.2 copy-start.4
  203.0 1.0 copy-start.1
  208.3 2.8 copy-start.14
  208.3 2.8 copy-start.18
  208.3 2.8 copy-start.21
  236.9 1.6 copy-start.10
  236.9 2.2 copy-start.13
  236.9 2.5 copy-start.22
  242.5 1.2 copy-start.5
  243.8 1.6 copy-start.2
  243.8 1.9 copy-start.3
  245.7 1.3 copy-start.6
  245.7 1.9 copy-start.7
  332.0 4.9 %copy-start = (bf16[2,1,5,32,4,16,128]{6,5,4,3,2,0,1:T(8,128)(2,1)}, bf16[2,1,5,32,4,16,128]{6,5,4,3,2,0,1:T(8,128)(2,1)S(1)}, u32[]{:S(2)}) copy-start(bf16[2,1,5,32,4,16,128]{6,5,4,3,2,0,1:T(8,128)(2,1)S(1)} %copy.164) | copy-start | bytes 15728644
  344.7 93.3 %collective-permute-start.3 = (bf16[2,1,4,128,16,128]{3,5,4,2,0,1:T(8,128)(2,1)}, bf16[2,1,4,128,16,128]{3,5,4,2,0,1:T(8,128)(2,1)}, u32[]{:S(2)}, u32[]{:S(2)}) collective-permute-start(bf16[2,1,4,128,16,128]{3,5,4,2,0,1:T(8,128)(2,1)} %copy.227), channel_id=1, source_target_pairs={{32,0},{64,32},{96,64},{33,1},{65,33},{97,65},{34,2},{66,34},{98,6... | collective-permute-start | bytes 12582920 | tf_op jit(solution)/shard_map/ppermute | solution.py:19
  357.3 94.8 %collective-permute-start.2 = (bf16[2,1,4,128,16,128]{3,5,4,2,0,1:T(8,128)(2,1)}, bf16[2,1,4,128,16,128]{3,5,4,2,0,1:T(8,128)(2,1)}, u32[]{:S(2)}, u32[]{:S(2)}) collective-permute-start(bf16[2,1,4,128,16,128]{3,5,4,2,0,1:T(8,128)(2,1)} %copy.226), channel_id=1, source_target_pairs={{0,32},{32,64},{64,96},{1,33},{33,65},{65,97},{2,34},{34,66},{66,9... | collective-permute-start | bytes 12582920 | tf_op jit(solution)/shard_map/ppermute | solution.py:17
where the time goes:
time: 485 us; the launch traced here: 478 us
  local copies, waits for them, and re-layouts  150 us (31%)
  waiting for transfers between devices  96.6 us (20%)
  other arithmetic  77.6 us (16%)
  blocking collectives  68.7 us (14%)
  matrix products  57.6 us (12%)
  starting transfers between devices  26.7 us (6%)
    unnamed x66, local copies, waits for them, and re-layouts  82.3 us
    ppermute x2, waiting for transfers between devices, extended(): lax.ppermute(head, axis, [((i + 1) % count, i) for i in range(ends)])  72.7 us
    all_to_all x1, blocking collectives, shards(): lax.all_to_all(half, ('col', 'en'), split_axis=4, concat_axis=3, tiled=True)  68.7 us
    another operation x8, other arithmetic  41.7 us
    ppermute x2, waiting for transfers between devices, extended(): lax.ppermute(tail, axis, [(i, (i + 1) % count) for i in range(ends)])  23.9 us
    dot_general x3, matrix products, shards(): jnp.einsum('xkamb,myf->xykabf', spread[:, :, slot], forward, preferred_el...  16.9 us
    convert_element_type x1, other arithmetic, shards(): return result.astype(jnp.bfloat16)  11.6 us
    unnamed x4, other arithmetic  11.5 us
  transfers between devices with their start and end apart: 6, of which 3 were waited for; matrix products, arithmetic and copies ran while one was open for 21% of the time, Pallas kernels for 0%

commit v1 on v0

v1 whole, which is shorter than its diff:
```python
import math

import jax
import jax.numpy as jnp
import ml_dtypes
import numpy as np
from jax import lax
from jax.experimental import pallas as pl
from jax.experimental.pallas import tpu as pltpu
from jax.sharding import PartitionSpec as P

MESH = pl.DeviceIdType.MESH
ORDER = (1, 0, 2)
FREQ = 384
LENGTH = 2 * FREQ


def tables(energies):
    freq = 2 * np.arange(FREQ)[:, None] + 1
    ahead = freq * np.arange(energies)[None, :] % (2 * LENGTH)
    back = (np.arange(energies) - energies // 2)[:, None] * freq.T % (2 * LENGTH)
    ahead = ahead * (math.pi / LENGTH)
    back = back * (math.pi / LENGTH)
    forward = np.concatenate([np.cos(ahead), np.sin(ahead)], axis=0)
    inverse = np.concatenate([np.cos(back), np.sin(back)], axis=1)
    return forward.astype(ml_dtypes.bfloat16), inverse.astype(ml_dtypes.bfloat16)


def kernel(
    lesser,
    greater,
    coupling,
    forward_hbm,
    inverse_hbm,
    out,
    forward,
    inverse,
    graw,
    turned,
    xin,
    yin,
    pout,
    own,
    near,
    total,
    swap,
    wide,
    left,
    right,
    xcat,
    ycat,
    spec_one,
    spec_two,
    product,
    staged,
    sem_local,
    sem_raw,
    sem_x,
    sem_y,
    sem_p,
    sem_n,
    sem_out,
):
    row = lax.axis_index("row")
    col = lax.axis_index("col")
    en = lax.axis_index("en")
    me = col * 8 + en
    below, above = lax.rem(row + 3, 4), lax.rem(row + 1, 4)

    def peer(step):
        index = lax.rem(me + step, 32)
        return index, (row, index // 8, lax.rem(index, 8))

    def local(src, dst, index):
        return pltpu.make_async_copy(src, dst, sem_local.at[index])

    barrier = pltpu.get_barrier_semaphore()

    def greet(step, carry):
        pl.semaphore_signal(barrier, inc=1, device_id=peer(step)[1], device_id_type=MESH)
        return carry

    load_raw = local(greater.at[:, 0, 1], graw.at[1], 0)
    load_raw.start()
    load_forward = local(forward_hbm, forward, 1)
    load_forward.start()
    load_inverse = local(inverse_hbm, inverse, 2)
    load_inverse.start()
    lax.fori_loop(1, 32, greet, 0)
    pl.semaphore_signal(barrier, inc=1, device_id=(below, col, en), device_id_type=MESH)
    pl.semaphore_signal(barrier, inc=1, device_id=(above, col, en), device_id_type=MESH)
    pl.semaphore_wait(barrier, 33)

    raw_down = pltpu.make_async_remote_copy(
        src_ref=greater.at[:, 0, 0],
        dst_ref=graw.at[2],
        send_sem=sem_raw.at[0],
        recv_sem=sem_raw.at[1],
        device_id=(below, col, en),
        device_id_type=MESH,
    )
    raw_up = pltpu.make_async_remote_copy(
        src_ref=greater.at[:, 0, 2],
        dst_ref=graw.at[0],
        send_sem=sem_raw.at[2],
        recv_sem=sem_raw.at[3],
        device_id=(above, col, en),
        device_id_type=MESH,
    )
    raw_down.start()
    raw_up.start()

    def send_x(slot):
        def body(step, carry):
            to = lax.rem(en + step, 8)
            pltpu.make_async_remote_copy(
                src_ref=lesser.at[:, 0, slot, pl.ds(4 * to, 4)],
                dst_ref=xin.at[slot, :, :, pl.ds(64 * en, 64), :],
                send_sem=sem_x.at[0, slot],
                recv_sem=sem_x.at[1, slot],
                device_id=(row, col, to),
                device_id_type=MESH,
            ).start()
            return carry

        lax.fori_loop(1, 8, body, 0)
        keep = local(
            lesser.at[:, 0, slot, pl.ds(4 * en, 4)],
            xin.at[slot, :, :, pl.ds(64 * en, 64), :],
            3 + slot,
        )
        keep.start()
        return keep

    def send_y(slot):
        def body(step, carry):
            index, target = peer(step)
            pltpu.make_async_remote_copy(
                src_ref=turned.at[slot, :, pl.ds(64 * index, 64), :],
                dst_ref=yin.at[slot, me],
                send_sem=sem_y.at[0, slot],
                recv_sem=sem_y.at[1, slot],
                device_id=target,
                device_id_type=MESH,
            ).start()
            return carry

        lax.fori_loop(1, 32, body, 0)
        keep = local(turned.at[slot, :, pl.ds(64 * me, 64), :], yin.at[slot, me], 6 + slot)
        keep.start()
        return keep

    def send_p(slot):
        def body(step, carry):
            index, target = peer(step)
            pltpu.make_async_remote_copy(
                src_ref=pout.at[slot, :, :, pl.ds(16 * index, 16), :],
                dst_ref=own.at[slot, :, pl.ds(4 * me, 4)],
                send_sem=sem_p.at[0, slot],
                recv_sem=sem_p.at[1, slot],
                device_id=target,
                device_id_type=MESH,
            ).start()
            return carry

        lax.fori_loop(1, 32, body, 0)
        keep = local(
            pout.at[slot, :, :, pl.ds(16 * me, 16), :],
            own.at[slot, :, pl.ds(4 * me, 4)],
            9 + slot,
        )
        keep.start()
        return keep

    def send_n(slot):
        copies = []
        for side, target in ((0, above), (1, below)):
            copy = pltpu.make_async_remote_copy(
                src_ref=own.at[slot],
                dst_ref=near.at[side, slot],
                send_sem=sem_n.at[0, side, slot],
                recv_sem=sem_n.at[1, side, slot],
                device_id=(target, col, en),
                device_id_type=MESH,
            )
            copy.start()
            copies.append(copy)
        return copies

    def bytes_of(ref, sem):
        pltpu.make_async_copy(ref, ref, sem).wait()

    def turn(slot):
        def part(p, carry):
            def one(s, inner):
                low = graw[slot, p, s]
                high = graw[slot, p, s + 16]
                square = jnp.concatenate([low, high], axis=0).astype(jnp.float32)
                swap[pl.ds(s, 128, stride=16), :] = square.T
                return inner

            lax.fori_loop(0, 16, one, 0)
            turned[slot, p] = swap[...].astype(jnp.bfloat16)
            return carry

        lax.fori_loop(0, 2, part, 0)

    lane = lax.broadcasted_iota(jnp.int32, (16, 128), 1)

    def correlate(slot):
        def body(a, carry):
            for p in range(2):
                xcat[:, p * 128 : (p + 1) * 128] = xin[slot, p, a]
            for p in range(2):
                for c in range(4):
                    for k in range(4):
                        one = yin[slot, c * 8 + 2 * k, p, pl.ds(16 * a, 16), :].astype(jnp.float32)
                        two = yin[slot, c * 8 + 2 * k + 1, p, pl.ds(16 * a, 16), :].astype(jnp.float32)
                        first = jnp.where(lane < 64, one, pltpu.roll(two, 64, 1))
                        second = jnp.where(lane < 64, pltpu.roll(one, 64, 1), two)
                        base = p * 128 + c * 32
                        ycat[base : base + 16, k * 128 : (k + 1) * 128] = first.astype(jnp.bfloat16)
                        ycat[base + 16 : base + 32, k * 128 : (k + 1) * 128] = second.astype(jnp.bfloat16)
            spec_one[...] = jnp.dot(forward[...], xcat[...], preferred_element_type=jnp.float32)
            spec_two[...] = lax.dot_general(
                forward[...], ycat[...], (((1,), (1,)), ((), ())), preferred_element_type=jnp.float32
            )

            def mix(step, inner):
                cos_rows = pl.ds(step * 16, 16)
                sin_rows = pl.ds(FREQ + step * 16, 16)
                one_rr, one_ri = spec_one[cos_rows, 0:128], spec_one[cos_rows, 128:256]
                one_sr, one_si = spec_one[sin_rows, 0:128], spec_one[sin_rows, 128:256]
                two_rr, two_ri = spec_two[cos_rows, 0:128], spec_two[cos_rows, 128:256]
                two_sr, two_si = spec_two[sin_rows, 0:128], spec_two[sin_rows, 128:256]
                a_re, a_im = one_rr + one_si, one_ri - one_sr
                a_re_m, a_im_m = one_rr - one_si, one_ri + one_sr
                b_re, b_im = two_rr - two_si, two_ri + two_sr
                b_re_m, b_im_m = two_rr + two_si, two_ri - two_sr
                s_re = a_re * b_re - a_im * b_im
                s_im = a_re * b_im + a_im * b_re
                s_re_m = a_re_m * b_re_m - a_im_m * b_im_m
                s_im_m = a_re_m * b_im_m + a_im_m * b_re_m
                product[cos_rows, 0:128] = (s_re + s_re_m).astype(jnp.bfloat16)
                product[sin_rows, 0:128] = (s_im_m - s_im).astype(jnp.bfloat16)
                product[cos_rows, 128:256] = (s_im + s_im_m).astype(jnp.bfloat16)
                product[sin_rows, 128:256] = (s_re - s_re_m).astype(jnp.bfloat16)
                return inner

            lax.fori_loop(0, FREQ // 16, mix, 0)
            lagged = jnp.dot(inverse[...], product[...], preferred_element_type=jnp.float32)
            scale = 1.0 / (LENGTH * 32.0)
            pout[slot, 0, a] = (scale * lagged[:, 128:256]).astype(jnp.bfloat16)
            pout[slot, 1, a] = (-scale * lagged[:, 0:128]).astype(jnp.bfloat16)
            return carry

        lax.fori_loop(0, 4, body, 0)

    def apply_left(tile_of, slot, side):
        column = side + slot

        def part(p, carry):
            swap[...] = tile_of(p).astype(jnp.float32).reshape(2048, 128)
            for pair in range(8):
                both = jnp.concatenate(
                    [
                        swap[pl.ds(2 * pair, 128, stride=16), :],
                        swap[pl.ds(2 * pair + 1, 128, stride=16), :],
                    ],
                    axis=1,
                ).astype(jnp.bfloat16)
                made = jnp.dot(left[side], both, preferred_element_type=jnp.float32)
                lower = pl.ds(256 * pair, 128)
                upper = pl.ds(256 * pair + 128, 128)
                total[p, column, lower, :] += made[:, 0:128]
                total[p, column, upper, :] += made[:, 128:256]
            return carry

        lax.fori_loop(0, 2, part, 0)

    waits = {}
    kept = {}
    kept["x", 1] = send_x(1)
    load_raw.wait()
    turn(1)
    kept["y", 1] = send_y(1)
    kept["x", 0] = send_x(0)
    kept["x", 2] = send_x(2)

    for side in range(3):
        inside = ((row + side - 1 >= 0) & (row + side - 1 < 4)).astype(jnp.float32)
        left[side] = (coupling[row, side].astype(jnp.float32) * inside).astype(jnp.bfloat16)
    for b in range(5):
        for s in range(5):
            block = (slice(b * 128, b * 128 + 128), slice(s * 128, s * 128 + 128))
            if abs(b - s) > 1:
                right[block] = jnp.zeros((128, 128), jnp.bfloat16)
            else:
                tile_b, tile_c = row + b - 2, row + s - 2
                inside = (
                    (tile_b >= 0) & (tile_b < 4) & (tile_c >= 0) & (tile_c < 4)
                ).astype(jnp.float32)
                safe = jnp.clip(tile_c, 0, 3)
                tile = coupling[safe, b - s + 1].astype(jnp.float32) * inside
                right[block] = tile.T.astype(jnp.bfloat16)

    def clear(step, carry):
        for b in range(5):
            total[0, b, pl.ds(step * 256, 256), :] = jnp.zeros((256, 128), jnp.float32)
            total[1, b, pl.ds(step * 256, 256), :] = jnp.zeros((256, 128), jnp.float32)
        return carry

    lax.fori_loop(0, 8, clear, 0)

    raw_up.wait_recv()
    turn(0)
    kept["y", 0] = send_y(0)
    load_forward.wait()
    load_inverse.wait()

    def arrive(slot):
        bytes_of(xin.at[slot, :, :, pl.ds(0, 448), :], sem_x.at[1, slot])
        kept["x", slot].wait()
        bytes_of(yin.at[slot, pl.ds(0, 31)], sem_y.at[1, slot])
        kept["y", slot].wait()

    def gather(slot):
        bytes_of(own.at[slot, :, pl.ds(0, 124)], sem_p.at[1, slot])
        kept["p", slot].wait()

    arrive(1)
    correlate(1)
    kept["p", 1] = send_p(1)
    raw_down.wait_recv()
    turn(2)
    kept["y", 2] = send_y(2)
    gather(1)
    waits[1] = send_n(1)
    apply_left(lambda p: own[1, p], 1, 1)
    arrive(0)
    correlate(0)
    kept["p", 0] = send_p(0)
    gather(0)
    waits[0] = send_n(0)
    apply_left(lambda p: own[0, p], 0, 1)
    arrive(2)
    correlate(2)
    kept["p", 2] = send_p(2)
    for side in range(2):
        waits[1][side].wait_recv()
        apply_left(lambda p: near[side, 1, p], 1, 2 * side)
    gather(2)
    waits[2] = send_n(2)
    apply_left(lambda p: own[2, p], 2, 1)
    for side in range(2):
        waits[0][side].wait_recv()
        apply_left(lambda p: near[side, 0, p], 0, 2 * side)
    for side in range(2):
        waits[2][side].wait_recv()
        apply_left(lambda p: near[side, 2, p], 2, 2 * side)

    for p in range(2):
        def finish(quad, carry):
            rows = pl.ds(quad * 512, 512)
            whole = jnp.concatenate(
                [total[p, b, rows, :].astype(jnp.bfloat16) for b in range(5)], axis=1
            )
            for s in range(5):
                low, high = max(s - 1, 0) * 128, min(s + 2, 5) * 128
                made = jnp.dot(
                    whole[:, low:high],
                    right[low:high, s * 128 : s * 128 + 128],
                    preferred_element_type=jnp.float32,
                )
                for lag in range(4):
                    wide[s, pl.ds(quad * 4 + lag, 128, stride=16), :] = made[lag * 128 : lag * 128 + 128]
            return carry

        lax.fori_loop(0, 4, finish, 0)
        for s in range(5):
            staged[p, s] = wide[s].astype(jnp.bfloat16).reshape(128, 16, 128)
        pltpu.make_async_copy(staged.at[p], out.at[p, 0], sem_out.at[p]).start()

    for p in range(2):
        pltpu.make_async_copy(staged.at[p], out.at[p, 0], sem_out.at[p]).wait()
    raw_down.wait_send()
    raw_up.wait_send()
    for slot in ORDER:
        bytes_of(xin.at[slot, :, :, pl.ds(0, 448), :], sem_x.at[0, slot])
        bytes_of(yin.at[slot, pl.ds(0, 31)], sem_y.at[0, slot])
        bytes_of(own.at[slot, :, pl.ds(0, 124)], sem_p.at[0, slot])
        for copy in waits[slot]:
            copy.wait_send()


def shards(lesser, greater, coupling):
    forward, inverse = tables(512)
    half = jnp.bfloat16
    whole = jnp.float32
    anywhere = pl.BlockSpec(memory_space=pl.ANY)
    return pl.pallas_call(
        kernel,
        out_shape=jax.ShapeDtypeStruct((2, 1, 5, 128, 16, 128), half),
        in_specs=[anywhere, anywhere, pl.BlockSpec(memory_space=pltpu.VMEM), anywhere, anywhere],
        out_specs=anywhere,
        scratch_shapes=[
            pltpu.VMEM((LENGTH, 512), half),
            pltpu.VMEM((512, LENGTH), half),
            pltpu.VMEM((3, 2, 32, 64, 128), half),
            pltpu.VMEM((3, 2, 2048, 128), half),
            pltpu.VMEM((3, 2, 4, 512, 128), half),
            pltpu.VMEM((3, 32, 2, 64, 128), half),
            pltpu.VMEM((3, 2, 4, 512, 128), half),
            pltpu.VMEM((3, 2, 128, 16, 128), half),
            pltpu.VMEM((2, 3, 2, 128, 16, 128), half),
            pltpu.VMEM((2, 5, 2048, 128), whole),
            pltpu.VMEM((2048, 128), whole),
            pltpu.VMEM((5, 2048, 128), whole),
            pltpu.VMEM((3, 128, 128), half),
            pltpu.VMEM((640, 640), half),
            pltpu.VMEM((512, 256), half),
            pltpu.VMEM((256, 512), half),
            pltpu.VMEM((LENGTH, 256), whole),
            pltpu.VMEM((LENGTH, 256), whole),
            pltpu.VMEM((LENGTH, 256), half),
            pltpu.VMEM((2, 5, 128, 16, 128), half),
            pltpu.SemaphoreType.DMA((12,)),
            pltpu.SemaphoreType.DMA((4,)),
            pltpu.SemaphoreType.DMA((2, 3)),
            pltpu.SemaphoreType.DMA((2, 3)),
            pltpu.SemaphoreType.DMA((2, 3)),
            pltpu.SemaphoreType.DMA((2, 2, 3)),
            pltpu.SemaphoreType.DMA((2,)),
        ],
        compiler_params=pltpu.CompilerParams(
            collective_id=0, has_side_effects=True, vmem_limit_bytes=60 * 1024 * 1024
        ),
        cost_estimate=pl.CostEstimate(flops=10**10, bytes_accessed=2 * 10**7, transcendentals=0),
    )(lesser, greater, coupling, jnp.asarray(forward), jnp.asarray(inverse))


def solution(mesh):
    placed = (P(None, "row", None, "col", "en", None), P(None, "row", None, "col", "en", None), P())
    return jax.shard_map(
        shards,
        mesh=mesh,
        in_specs=placed,
        out_specs=P(None, "row", None, None, ("col", "en"), None),
        check_vma=False,
    )
```

time: 485 us -> 180 us (0.37)
  the two profiles are of different devices: /device:TPU:24 before, /device:TPU:9 now
where the time goes in v1:
time: 180 us; the launch traced here: 176 us
  Pallas kernels  171 us (95%)
  local copies, waits for them, and re-layouts  5.79 us (3%)
    pallas_call x1, Pallas kernels, shards(): pl.pallas_call(kernel, out_shape=jax.ShapeDtypeStruct((2, 1, 5, 128, 16,...  171 us
    unnamed x1, local copies, waits for them, and re-layouts  5.79 us

profile of v1, /device:TPU:9, one launch (start us, length us, event | category | flops | bytes accessed | tf_op | source)
XLA Modules:
  0.0 176.5 jit_solution(1605731303333790755)
XLA Ops:
  0.0 170.7 %shard_map.55 = bf16[2,1,5,128,16,128]{5,4,3,2,1,0:T(8,128)(2,1)} custom-call(bf16[2,1,3,32,64,128]{5,4,3,2,1,0:T(8,128)(2,1)} %lesser.1, bf16[2,1,3,32,64,128]{5,4,3,2,1,0:T(8,128)(2,1)} %greater.1, bf16[4,3,128,128]{3,2,1,0:T(8,128)(2,1)} %coupling.1, bf16[768,512]{1,0:T(8,128)(2,1)} %constant.4.clone.forward_hbm, bf16[512,768]{1,0:T(8,128)(2,1)} %constant.5.clone.inverse_hbm), custom_call_target="tpu_custom_call" | custom-call | flops 10000000000 | bytes 20000000 | tf_op jit(solution)/shard_map/pallas_call | solution.py:401
  170.7 5.8 %copy.7 = bf16[2,1,5,128,16,128]{5,4,3,2,1,0:T(8,128)(2,1)} copy(bf16[2,1,5,128,16,128]{5,4,3,2,1,0:T(8,128)(2,1)} %shard_map.55) | data formatting | bytes 10485760

commit v2 on v1

v2 whole, which is shorter than its diff:
```python
import math

import jax
import jax.numpy as jnp
import ml_dtypes
import numpy as np
from jax import lax
from jax.experimental import pallas as pl
from jax.experimental.pallas import tpu as pltpu
from jax.sharding import PartitionSpec as P

MESH = pl.DeviceIdType.MESH
DIAG, INWARD, SHARED = 0, 1, 2
FREQ = 384
LENGTH = 2 * FREQ


def tables(energies):
    freq = 2 * np.arange(FREQ)[:, None] + 1
    ahead = freq * np.arange(energies)[None, :] % (2 * LENGTH)
    back = (np.arange(energies) - energies // 2)[:, None] * freq.T % (2 * LENGTH)
    ahead = ahead * (math.pi / LENGTH)
    back = back * (math.pi / LENGTH)
    forward = np.concatenate([np.cos(ahead), np.sin(ahead)], axis=0)
    inverse = np.concatenate([np.cos(back), np.sin(back)], axis=1)
    return forward.astype(ml_dtypes.bfloat16), inverse.astype(ml_dtypes.bfloat16)


CHUNKS = ((DIAG, 0), (DIAG, 1), (SHARED, None), (INWARD, 0), (INWARD, 1))
D0, D1, S, I0, I1 = range(5)


def kernel(
    lesser,
    greater,
    coupling,
    forward_hbm,
    inverse_hbm,
    out,
    forward,
    inverse,
    graw,
    turned,
    xpass,
    ypass,
    xin,
    yin,
    pout,
    own,
    nearby,
    across,
    total,
    swap,
    wide,
    left,
    right,
    xcat,
    ycat,
    spec_one,
    spec_two,
    product,
    staged,
    sem_load,
    sem_keep,
    sem_raw,
    sem_pass,
    sem_x,
    sem_y,
    sem_p,
    sem_near,
    sem_across,
    sem_far,
    sem_out,
):
    row = lax.axis_index("row")
    col = lax.axis_index("col")
    en = lax.axis_index("en")
    me = col * 8 + en
    partner = row + 1 - 2 * lax.rem(row, 2)
    other = 3 - row
    far = lax.rem(row + 2, 4)
    inward = 1 - 2 * (row // 2)
    inner = lax.rem(lax.rem(row, 2) + row // 2, 2)
    is_inner = inner == 1
    is_outer = inner == 0
    slot_in, slot_out = 1 + inward, 1 - inward

    def peer(step):
        index = lax.rem(me + step, 32)
        return index, (row, index // 8, lax.rem(index, 8))

    def remote(src, dst, send, recv, target):
        return pltpu.make_async_remote_copy(
            src_ref=src,
            dst_ref=dst,
            send_sem=send,
            recv_sem=recv,
            device_id=target,
            device_id_type=MESH,
        )

    def across_rows(target):
        return (target, col, en)

    def bytes_of(ref, sem):
        pltpu.make_async_copy(ref, ref, sem).wait()

    load_diag = pltpu.make_async_copy(greater.at[:, 1], graw.at[DIAG], sem_load.at[0])
    load_forward = pltpu.make_async_copy(forward_hbm, forward, sem_load.at[1])
    load_inverse = pltpu.make_async_copy(inverse_hbm, inverse, sem_load.at[2])
    load_diag.start()

    @pl.when(is_outer)
    def _():
        pltpu.make_async_copy(greater.at[:, slot_in], graw.at[SHARED], sem_load.at[3]).start()

    @pl.when(is_inner)
    def _():
        pltpu.make_async_copy(lesser.at[:, slot_out, :, pl.ds(2, 2)], xpass, sem_load.at[4]).start()

    load_forward.start()
    load_inverse.start()

    barrier = pltpu.get_barrier_semaphore()

    def greet(step, carry):
        pl.semaphore_signal(barrier, inc=1, device_id=peer(step)[1], device_id_type=MESH)
        return carry

    lax.fori_loop(1, 32, greet, 0)
    for step in range(1, 4):
        pl.semaphore_signal(
            barrier, inc=1, device_id=across_rows(lax.rem(row + step, 4)), device_id_type=MESH
        )
    pl.semaphore_wait(barrier, 34)

    @pl.when(is_inner)
    def _():
        remote(
            lesser.at[:, slot_out, :, pl.ds(0, 2)], xpass, sem_pass.at[0], sem_pass.at[1], across_rows(partner)
        ).start()
        remote(
            greater.at[:, slot_out], graw.at[INWARD], sem_raw.at[0], sem_raw.at[2], across_rows(partner)
        ).start()
        remote(
            greater.at[:, slot_in], graw.at[INWARD], sem_raw.at[1], sem_raw.at[2], across_rows(other)
        ).start()

    def send_x(chunk):
        kind, half = CHUNKS[chunk]

        def source(to):
            if kind == SHARED:
                return xpass.at[:, to]
            return lesser.at[:, 1 if kind == DIAG else slot_in, to, pl.ds(2 * half, 2)]

        place = xin.at[chunk, :, :, pl.ds(64 * en, 64), :]

        def body(step, carry):
            to = lax.rem(en + step, 8)
            remote(source(to), place, sem_x.at[0, chunk], sem_x.at[1, chunk], (row, col, to)).start()
            return carry

        lax.fori_loop(1, 8, body, 0)
        pltpu.make_async_copy(source(en), place, sem_keep.at[0, chunk]).start()

    def send_y(chunk):
        kind, half = CHUNKS[chunk]

        def source(index):
            if kind == SHARED:
                return ypass.at[:, index]
            return turned.at[kind, :, index, pl.ds(32 * half, 32), :]

        def body(step, carry):
            index, target = peer(step)
            remote(
                source(index), yin.at[chunk, me], sem_y.at[0, chunk], sem_y.at[1, chunk], target
            ).start()
            return carry

        lax.fori_loop(1, 32, body, 0)
        pltpu.make_async_copy(source(me), yin.at[chunk, me], sem_keep.at[1, chunk]).start()

    def first_row(chunk):
        half = CHUNKS[chunk][1]
        return 2 * inner if half is None else 2 * half

    def parts_of(chunk):
        return ((0, 1), (1, 1)) if chunk == I1 else ((0, 2),)

    def send_p(chunk):
        kind = CHUNKS[chunk][0]
        for p, count in parts_of(chunk):
            place = own.at[kind, pl.ds(p, count), pl.ds(first_row(chunk), 2), me]

            def body(step, carry):
                index, target = peer(step)
                remote(
                    pout.at[chunk, pl.ds(p, count), :, pl.ds(16 * index, 16), :],
                    place,
                    sem_p.at[0, chunk, p],
                    sem_p.at[1, chunk, p],
                    target,
                ).start()
                return carry

            lax.fori_loop(1, 32, body, 0)
            pltpu.make_async_copy(
                pout.at[chunk, pl.ds(p, count), :, pl.ds(16 * me, 16), :], place, sem_keep.at[2 + p, chunk]
            ).start()

    def arrive(chunk):
        bytes_of(xin.at[chunk, :, :, pl.ds(0, 448), :], sem_x.at[1, chunk])
        bytes_of(xin.at[chunk, :, :, pl.ds(0, 64), :], sem_keep.at[0, chunk])
        bytes_of(yin.at[chunk, pl.ds(0, 31)], sem_y.at[1, chunk])
        bytes_of(yin.at[chunk, 0], sem_keep.at[1, chunk])

    def gather(chunk):
        kind = CHUNKS[chunk][0]
        for p, count in parts_of(chunk):
            bytes_of(own.at[kind, pl.ds(p, count), pl.ds(0, 2), pl.ds(0, 31)], sem_p.at[1, chunk, p])
            bytes_of(own.at[kind, pl.ds(p, count), pl.ds(0, 2), 0], sem_keep.at[2 + p, chunk])
            rows = pl.ds(first_row(chunk), 2)
            src = own.at[kind, pl.ds(p, count), rows]
            dst = src if kind == SHARED else nearby.at[kind, pl.ds(p, count), rows]
            remote(
                src, dst, sem_near.at[0, chunk, p], sem_near.at[1, chunk, p], across_rows(partner)
            ).start()

            @pl.when(is_inner)
            def _():
                remote(
                    src,
                    across.at[kind, pl.ds(p, count), rows],
                    sem_across.at[0, chunk, p],
                    sem_across.at[1, chunk, p],
                    across_rows(other),
                ).start()

            if chunk == S:

                @pl.when(is_outer)
                def _():
                    remote(
                        src, across.at[kind, :, pl.ds(0, 2)], sem_far.at[0], sem_far.at[1], across_rows(far)
                    ).start()

    def chunk_bytes(chunk, p, count):
        return own.at[CHUNKS[chunk][0], pl.ds(p, count), pl.ds(0, 2)]

    def from_partner(chunk, p):
        bytes_of(chunk_bytes(chunk, p, dict(parts_of(chunk))[p]), sem_near.at[1, chunk, p])

    def from_other(chunk, p):
        bytes_of(chunk_bytes(chunk, p, dict(parts_of(chunk))[p]), sem_across.at[1, chunk, p])

    def turn(kind):
        def part(p, carry):
            def one(s, inside):
                square = jnp.concatenate([graw[kind, p, s], graw[kind, p, s + 16]], axis=0).astype(jnp.float32)
                swap[pl.ds(s, 128, stride=16), :] = square.T
                return inside

            lax.fori_loop(0, 16, one, 0)
            turned[kind, p] = swap[...].astype(jnp.bfloat16).reshape(32, 64, 128)
            return carry

        lax.fori_loop(0, 2, part, 0)

    lane = lax.broadcasted_iota(jnp.int32, (16, 128), 1)

    def correlate(chunk):
        def body(a, carry):
            for p in range(2):
                xcat[:, p * 128 : (p + 1) * 128] = xin[chunk, p, a]
            for p in range(2):
                for c in range(4):
                    for k in range(4):
                        one = yin[chunk, c * 8 + 2 * k, p, pl.ds(16 * a, 16), :].astype(jnp.float32)
                        two = yin[chunk, c * 8 + 2 * k + 1, p, pl.ds(16 * a, 16), :].astype(jnp.float32)
                        first = jnp.where(lane < 64, one, pltpu.roll(two, 64, 1))
                        second = jnp.where(lane < 64, pltpu.roll(one, 64, 1), two)
                        base = p * 128 + c * 32
                        ycat[base : base + 16, k * 128 : (k + 1) * 128] = first.astype(jnp.bfloat16)
                        ycat[base + 16 : base + 32, k * 128 : (k + 1) * 128] = second.astype(jnp.bfloat16)
            spec_one[...] = jnp.dot(forward[...], xcat[...], preferred_element_type=jnp.float32)
            spec_two[...] = lax.dot_general(
                forward[...], ycat[...], (((1,), (1,)), ((), ())), preferred_element_type=jnp.float32
            )

            def mix(step, inner):
                cos_rows = pl.ds(step * 16, 16)
                sin_rows = pl.ds(FREQ + step * 16, 16)
                one_rr, one_ri = spec_one[cos_rows, 0:128], spec_one[cos_rows, 128:256]
                one_sr, one_si = spec_one[sin_rows, 0:128], spec_one[sin_rows, 128:256]
                two_rr, two_ri = spec_two[cos_rows, 0:128], spec_two[cos_rows, 128:256]
                two_sr, two_si = spec_two[sin_rows, 0:128], spec_two[sin_rows, 128:256]
                a_re, a_im = one_rr + one_si, one_ri - one_sr
                a_re_m, a_im_m = one_rr - one_si, one_ri + one_sr
                b_re, b_im = two_rr - two_si, two_ri + two_sr
                b_re_m, b_im_m = two_rr + two_si, two_ri - two_sr
                s_re = a_re * b_re - a_im * b_im
                s_im = a_re * b_im + a_im * b_re
                s_re_m = a_re_m * b_re_m - a_im_m * b_im_m
                s_im_m = a_re_m * b_im_m + a_im_m * b_re_m
                product[cos_rows, 0:128] = (s_re + s_re_m).astype(jnp.bfloat16)
                product[sin_rows, 0:128] = (s_im_m - s_im).astype(jnp.bfloat16)
                product[cos_rows, 128:256] = (s_im + s_im_m).astype(jnp.bfloat16)
                product[sin_rows, 128:256] = (s_re - s_re_m).astype(jnp.bfloat16)
                return inner

            lax.fori_loop(0, FREQ // 16, mix, 0)
            lagged = jnp.dot(inverse[...], product[...], preferred_element_type=jnp.float32)
            scale = 1.0 / (LENGTH * 32.0)
            pout[chunk, 0, a] = (scale * lagged[:, 128:256]).astype(jnp.bfloat16)
            pout[chunk, 1, a] = (-scale * lagged[:, 0:128]).astype(jnp.bfloat16)
            return carry

        lax.fori_loop(0, 2, body, 0)

    def apply_left(tile, side, column, parts=(0, 2)):
        def part(p, carry):
            swap[...] = tile[p].astype(jnp.float32).reshape(2048, 128)
            for pair in range(8):
                both = jnp.concatenate(
                    [
                        swap[pl.ds(2 * pair, 128, stride=16), :],
                        swap[pl.ds(2 * pair + 1, 128, stride=16), :],
                    ],
                    axis=1,
                ).astype(jnp.bfloat16)
                made = jnp.dot(left[side], both, preferred_element_type=jnp.float32)
                lower = pl.ds(256 * pair, 128)
                upper = pl.ds(256 * pair + 128, 128)
                total[p, column, lower, :] += made[:, 0:128]
                total[p, column, upper, :] += made[:, 128:256]
            return carry

        lax.fori_loop(*parts, part, 0)

    def finish(p):
        def block(quad, carry):
            rows = pl.ds(quad * 512, 512)
            whole = jnp.concatenate([total[p, b, rows, :].astype(jnp.bfloat16) for b in range(5)], axis=1)
            for s in range(5):
                low, high = max(s - 1, 0) * 128, min(s + 2, 5) * 128
                made = jnp.dot(
                    whole[:, low:high],
                    right[low:high, s * 128 : s * 128 + 128],
                    preferred_element_type=jnp.float32,
                )
                for lag in range(4):
                    wide[s, pl.ds(quad * 4 + lag, 128, stride=16), :] = made[lag * 128 : lag * 128 + 128]
            return carry

        lax.fori_loop(0, 4, block, 0)
        for s in range(5):
            staged[p, s] = wide[s].astype(jnp.bfloat16).reshape(128, 16, 128)
        pltpu.make_async_copy(staged.at[p], out.at[p, 0], sem_out.at[p]).start()

    send_x(D0)
    load_diag.wait()
    turn(DIAG)
    send_y(D0)
    send_x(D1)
    send_y(D1)

    @pl.when(is_outer)
    def _():
        bytes_of(graw.at[SHARED], sem_load.at[3])
        turn(SHARED)
        pltpu.make_async_copy(turned.at[SHARED, :, :, pl.ds(0, 32), :], ypass, sem_load.at[5]).start()
        remote(
            turned.at[SHARED, :, :, pl.ds(32, 32), :], ypass, sem_pass.at[2], sem_pass.at[3], across_rows(partner)
        ).start()

    place = lax.broadcasted_iota(jnp.int32, (128, 128), 1)
    orbital = lax.broadcasted_iota(jnp.int32, (128, 128), 0)
    order = (orbital == 4 * lax.rem(place, 32) + place // 32).astype(jnp.bfloat16)
    for side in range(3):
        left[side] = jnp.dot(coupling[row, side], order, preferred_element_type=jnp.float32).astype(jnp.bfloat16)
    for b in range(5):
        for s in range(max(b - 1, 0), min(b + 2, 5)):
            block = (slice(b * 128, b * 128 + 128), slice(s * 128, s * 128 + 128))
            tile_b, tile_c = row + b - 2, row + s - 2
            inside = ((tile_b >= 0) & (tile_b < 4) & (tile_c >= 0) & (tile_c < 4)).astype(jnp.float32)
            safe = jnp.clip(tile_c, 0, 3)
            tile = coupling[safe, b - s + 1].astype(jnp.float32) * inside
            right[block] = tile.T.astype(jnp.bfloat16)

    def clear(step, carry):
        for b in range(5):
            total[0, b, pl.ds(step * 256, 256), :] = jnp.zeros((256, 128), jnp.float32)
            total[1, b, pl.ds(step * 256, 256), :] = jnp.zeros((256, 128), jnp.float32)
        return carry

    lax.fori_loop(0, 8, clear, 0)
    load_forward.wait()
    load_inverse.wait()

    arrive(D0)
    correlate(D0)
    send_p(D0)

    @pl.when(is_outer)
    def _():
        bytes_of(xpass, sem_pass.at[1])
        bytes_of(ypass, sem_load.at[5])

    @pl.when(is_inner)
    def _():
        bytes_of(xpass, sem_load.at[4])
        bytes_of(ypass, sem_pass.at[3])

    send_x(S)
    send_y(S)
    bytes_of(graw.at[INWARD], sem_raw.at[2])
    turn(INWARD)
    arrive(D1)
    correlate(D1)
    send_p(D1)
    send_x(I0)
    send_y(I0)
    gather(D0)
    arrive(S)
    correlate(S)
    send_p(S)
    send_x(I1)
    send_y(I1)
    gather(D1)
    apply_left(own.at[DIAG], 1, 2)
    arrive(I0)
    correlate(I0)
    send_p(I0)
    gather(S)
    arrive(I1)
    correlate(I1)
    send_p(I1)
    gather(I0)

    toward = inward * (1 - 2 * inner)
    from_partner(D0, 0)
    from_partner(D1, 0)
    apply_left(nearby.at[DIAG], 1 + toward, 2 + toward)

    @pl.when(is_inner)
    def _():
        from_other(D0, 0)
        from_other(D1, 0)
        apply_left(across.at[DIAG], 1 + inward, 2 + inward)

    gather(I1)
    from_partner(S, 0)
    apply_left(own.at[SHARED], 1 + inward * (1 - inner), 2 - inward * inner)
    apply_left(own.at[INWARD], 1, 2 + inward)

    @pl.when(is_inner)
    def _():
        from_other(S, 0)
        bytes_of(chunk_bytes(S, 0, 2), sem_far.at[1])
        apply_left(across.at[SHARED], 1 + inward, 2 + 2 * inward)

    from_partner(I0, 0)

    @pl.when(is_inner)
    def _():
        from_other(I0, 0)

    for p in range(2):
        from_partner(I1, p)
        apply_left(nearby.at[INWARD], 1 + toward, 2 + 2 * inward * (1 - inner), (p, p + 1))

        @pl.when(is_inner)
        def _():
            from_other(I1, p)
            apply_left(across.at[INWARD], 1 + inward, 2, (p, p + 1))

        finish(p)

    for p in range(2):
        pltpu.make_async_copy(staged.at[p], out.at[p, 0], sem_out.at[p]).wait()

    @pl.when(is_inner)
    def _():
        bytes_of(xpass, sem_pass.at[0])
        bytes_of(graw.at[INWARD], sem_raw.at[0])
        bytes_of(graw.at[INWARD], sem_raw.at[1])

    @pl.when(is_outer)
    def _():
        bytes_of(ypass, sem_pass.at[2])
        bytes_of(chunk_bytes(S, 0, 2), sem_far.at[0])

    for chunk in range(5):
        kind = CHUNKS[chunk][0]
        bytes_of(xin.at[chunk, :, :, pl.ds(0, 448), :], sem_x.at[0, chunk])
        bytes_of(yin.at[chunk, pl.ds(0, 31)], sem_y.at[0, chunk])
        for p, count in parts_of(chunk):
            bytes_of(own.at[kind, pl.ds(p, count), pl.ds(0, 2), pl.ds(0, 31)], sem_p.at[0, chunk, p])
            bytes_of(chunk_bytes(chunk, p, count), sem_near.at[0, chunk, p])

            @pl.when(is_inner)
            def _():
                bytes_of(chunk_bytes(chunk, p, count), sem_across.at[0, chunk, p])


def shards(lesser, greater, coupling):
    forward, inverse = tables(512)
    half = jnp.bfloat16
    whole = jnp.float32
    anywhere = pl.BlockSpec(memory_space=pl.ANY)
    return pl.pallas_call(
        kernel,
        out_shape=jax.ShapeDtypeStruct((2, 1, 5, 128, 16, 128), half),
        in_specs=[anywhere, anywhere, pl.BlockSpec(memory_space=pltpu.VMEM), anywhere, anywhere],
        out_specs=anywhere,
        scratch_shapes=[
            pltpu.VMEM((LENGTH, 512), half),
            pltpu.VMEM((512, LENGTH), half),
            pltpu.VMEM((3, 2, 32, 64, 128), half),
            pltpu.VMEM((3, 2, 32, 64, 128), half),
            pltpu.VMEM((2, 8, 2, 64, 128), half),
            pltpu.VMEM((2, 32, 32, 128), half),
            pltpu.VMEM((5, 2, 2, 512, 128), half),
            pltpu.VMEM((5, 32, 2, 32, 128), half),
            pltpu.VMEM((5, 2, 2, 512, 128), half),
            pltpu.VMEM((3, 2, 4, 32, 16, 128), half),
            pltpu.VMEM((2, 2, 4, 32, 16, 128), half),
            pltpu.VMEM((3, 2, 4, 32, 16, 128), half),
            pltpu.VMEM((2, 5, 2048, 128), whole),
            pltpu.VMEM((2048, 128), whole),
            pltpu.VMEM((5, 2048, 128), whole),
            pltpu.VMEM((3, 128, 128), half),
            pltpu.VMEM((640, 640), half),
            pltpu.VMEM((512, 256), half),
            pltpu.VMEM((256, 512), half),
            pltpu.VMEM((LENGTH, 256), whole),
            pltpu.VMEM((LENGTH, 256), whole),
            pltpu.VMEM((LENGTH, 256), half),
            pltpu.VMEM((2, 5, 128, 16, 128), half),
            pltpu.SemaphoreType.DMA((6,)),
            pltpu.SemaphoreType.DMA((4, 5)),
            pltpu.SemaphoreType.DMA((3,)),
            pltpu.SemaphoreType.DMA((4,)),
            pltpu.SemaphoreType.DMA((2, 5)),
            pltpu.SemaphoreType.DMA((2, 5)),
            pltpu.SemaphoreType.DMA((2, 5, 2)),
            pltpu.SemaphoreType.DMA((2, 5, 2)),
            pltpu.SemaphoreType.DMA((2, 5, 2)),
            pltpu.SemaphoreType.DMA((2,)),
            pltpu.SemaphoreType.DMA((2,)),
        ],
        compiler_params=pltpu.CompilerParams(
            collective_id=0, has_side_effects=True, vmem_limit_bytes=60 * 1024 * 1024
        ),
        cost_estimate=pl.CostEstimate(flops=10**10, bytes_accessed=2 * 10**7, transcendentals=0),
    )(
        lesser.reshape(2, 3, 8, 4, 64, 128),
        greater.reshape(2, 3, 32, 64, 128),
        coupling,
        jnp.asarray(forward),
        jnp.asarray(inverse),
    )


def solution(mesh):
    placed = (P(None, "row", None, "col", "en", None), P(None, "row", None, "col", "en", None), P())
    return jax.shard_map(
        shards,
        mesh=mesh,
        in_specs=placed,
        out_specs=P(None, "row", None, None, ("col", "en"), None),
        check_vma=False,
    )
```

time: 180 us -> 144 us (0.80); the launches traced: 176 us -> 143 us
  Pallas kernels: 171 us -> 137 us
    pallas_call x1, Pallas kernels: 171 us -> 137 us  [shards(): pl.pallas_call(kernel, out_shape=jax.ShapeDtypeStruct((2, 1, 5, 128, 16,...]
where the time goes in v2:
time: 144 us; the launch traced here: 143 us
  Pallas kernels  137 us (95%)
  local copies, waits for them, and re-layouts  5.79 us (4%)
    pallas_call x1, Pallas kernels, shards(): pl.pallas_call(kernel, out_shape=jax.ShapeDtypeStruct((2, 1, 5, 128, 16,...  137 us
    unnamed x1, local copies, waits for them, and re-layouts  5.79 us

profile of v2, /device:TPU:9, one launch (start us, length us, event | category | flops | bytes accessed | tf_op | source)
XLA Modules:
  0.0 143.0 jit_solution(18315902287134373558)
XLA Ops:
  0.0 137.2 %shard_map.55 = bf16[2,1,5,128,16,128]{5,4,3,2,1,0:T(8,128)(2,1)} custom-call(bf16[2,3,8,4,64,128]{5,4,3,2,1,0:T(8,128)(2,1)} %bitcast.2, bf16[2,3,32,64,128]{4,3,2,1,0:T(8,128)(2,1)} %bitcast.3, bf16[4,3,128,128]{3,2,1,0:T(8,128)(2,1)} %coupling.1, bf16[768,512]{1,0:T(8,128)(2,1)} %constant.4.clone.forward_hbm, bf16[512,768]{1,0:T(8,128)(2,1)} %constant.5.clone.inverse_hbm), custom_call_target="tpu_custom_call" | custom-call | flops 10000000000 | bytes 20000000 | tf_op jit(solution)/shard_map/pallas_call | solution.py:513
  137.2 5.8 %copy.7 = bf16[2,1,5,128,16,128]{5,4,3,2,1,0:T(8,128)(2,1)} copy(bf16[2,1,5,128,16,128]{5,4,3,2,1,0:T(8,128)(2,1)} %shard_map.55) | data formatting | bytes 10485760

commit v3 on v2

v3 whole, which is shorter than its diff:
```python
import math

import jax
import jax.numpy as jnp
import ml_dtypes
import numpy as np
from jax import lax
from jax.experimental import pallas as pl
from jax.experimental.pallas import tpu as pltpu
from jax.sharding import PartitionSpec as P

MESH = pl.DeviceIdType.MESH
DIAG, INWARD, SHARED = 0, 1, 2
FREQ = 384
LENGTH = 2 * FREQ


def tables(energies):
    freq = 2 * np.arange(FREQ)[:, None] + 1
    ahead = freq * np.arange(energies)[None, :] % (2 * LENGTH)
    back = (np.arange(energies) - energies // 2)[:, None] * freq.T % (2 * LENGTH)
    ahead = ahead * (math.pi / LENGTH)
    back = back * (math.pi / LENGTH)
    forward = np.concatenate([np.cos(ahead), np.sin(ahead)], axis=0)
    inverse = np.concatenate([np.cos(back), np.sin(back)], axis=1)
    return forward.astype(ml_dtypes.bfloat16), inverse.astype(ml_dtypes.bfloat16)


CHUNKS = 10
AHEAD = 2


def kernel(
    lesser,
    greater,
    coupling,
    forward_hbm,
    inverse_hbm,
    out,
    forward,
    inverse,
    graw,
    turned,
    xpass,
    ypass,
    xin,
    yin,
    pout,
    own,
    nearby,
    across,
    total,
    swap,
    swap_two,
    mixed,
    wide,
    left,
    right,
    right_last,
    xcat,
    ycat,
    spec_one,
    spec_two,
    product,
    staged,
    sem_load,
    sem_keep,
    sem_raw,
    sem_pass,
    sem_x,
    sem_y,
    sem_p,
    sem_near,
    sem_across,
    sem_far,
    sem_out,
):
    row = lax.axis_index("row")
    col = lax.axis_index("col")
    en = lax.axis_index("en")
    me = col * 8 + en
    partner = row + 1 - 2 * lax.rem(row, 2)
    other = 3 - row
    far = lax.rem(row + 2, 4)
    inward = 1 - 2 * (row // 2)
    inner = lax.rem(lax.rem(row, 2) + row // 2, 2)
    is_inner = inner == 1
    is_outer = inner == 0
    slot_in, slot_out = 1 + inward, 1 - inward
    toward = inward * (1 - 2 * inner)
    last = 2 + 2 * inward * (1 - inner)

    def peer(step):
        index = lax.rem(me + step, 32)
        return index, (row, index // 8, lax.rem(index, 8))

    def remote(src, dst, send, recv, target):
        return pltpu.make_async_remote_copy(
            src_ref=src,
            dst_ref=dst,
            send_sem=send,
            recv_sem=recv,
            device_id=target,
            device_id_type=MESH,
        )

    def across_rows(target):
        return (target, col, en)

    def bytes_of(ref, sem):
        pltpu.make_async_copy(ref, ref, sem).wait()

    load_diag = pltpu.make_async_copy(greater.at[:, 1], graw.at[DIAG], sem_load.at[0])
    load_forward = pltpu.make_async_copy(forward_hbm, forward, sem_load.at[1])
    load_inverse = pltpu.make_async_copy(inverse_hbm, inverse, sem_load.at[2])
    load_diag.start()

    @pl.when(is_outer)
    def _():
        pltpu.make_async_copy(greater.at[:, slot_in], graw.at[SHARED], sem_load.at[3]).start()

    @pl.when(is_inner)
    def _():
        pltpu.make_async_copy(lesser.at[:, slot_out, :, pl.ds(2, 2)], xpass, sem_load.at[4]).start()

    load_forward.start()
    load_inverse.start()

    barrier = pltpu.get_barrier_semaphore()

    def greet(step, carry):
        pl.semaphore_signal(barrier, inc=1, device_id=peer(step)[1], device_id_type=MESH)
        return carry

    lax.fori_loop(1, 32, greet, 0)
    for step in range(1, 4):
        pl.semaphore_signal(
            barrier, inc=1, device_id=across_rows(lax.rem(row + step, 4)), device_id_type=MESH
        )
    pl.semaphore_wait(barrier, 34)

    @pl.when(is_inner)
    def _():
        remote(
            lesser.at[:, slot_out, :, pl.ds(0, 2)], xpass, sem_pass.at[0], sem_pass.at[1], across_rows(partner)
        ).start()
        remote(
            greater.at[:, slot_out], graw.at[INWARD], sem_raw.at[0], sem_raw.at[2], across_rows(partner)
        ).start()
        remote(
            greater.at[:, slot_in], graw.at[INWARD], sem_raw.at[1], sem_raw.at[2], across_rows(other)
        ).start()

    def is_kind(chunk, kind):
        if kind == DIAG:
            return chunk < 4
        if kind == SHARED:
            return (chunk >= 4) & (chunk < 6)
        return chunk >= 6

    def place_of(chunk):
        shared = (chunk >= 4).astype(jnp.int32) - (chunk >= 6).astype(jnp.int32)
        return chunk + 2 * inner * shared + 2 * (chunk >= 6).astype(jnp.int32)

    def send_x(chunk):
        place = xin.at[chunk, :, pl.ds(64 * en, 64), :]

        def spread(source):
            def body(step, carry):
                to = lax.rem(en + step, 8)
                remote(source(to), place, sem_x.at[0, chunk], sem_x.at[1, chunk], (row, col, to)).start()
                return carry

            lax.fori_loop(1, 8, body, 0)
            pltpu.make_async_copy(source(en), place, sem_keep.at[0, chunk]).start()

        @pl.when(is_kind(chunk, SHARED))
        def _():
            spread(lambda to: xpass.at[:, to, chunk - 4])

        @pl.when(jnp.logical_not(is_kind(chunk, SHARED)))
        def _():
            inside = (chunk >= 6).astype(jnp.int32)
            spread(lambda to: lesser.at[:, 1 + inside * inward, to, chunk - 6 * inside])

    def send_y(chunk):
        place = yin.at[chunk, me]

        def spread(source):
            def body(step, carry):
                index, target = peer(step)
                remote(source(index), place, sem_y.at[0, chunk], sem_y.at[1, chunk], target).start()
                return carry

            lax.fori_loop(1, 32, body, 0)
            pltpu.make_async_copy(source(me), place, sem_keep.at[1, chunk]).start()

        @pl.when(is_kind(chunk, SHARED))
        def _():
            spread(lambda index: ypass.at[:, index, pl.ds(16 * (chunk - 4), 16), :])

        @pl.when(jnp.logical_not(is_kind(chunk, SHARED)))
        def _():
            inside = (chunk >= 6).astype(jnp.int32)
            spread(lambda index: turned.at[inside, :, index, pl.ds(16 * (chunk - 6 * inside), 16), :])

    def send_p(chunk):
        place = own.at[place_of(chunk), :, me]

        def body(step, carry):
            index, target = peer(step)
            remote(
                pout.at[chunk, :, pl.ds(16 * index, 16), :], place, sem_p.at[0, chunk], sem_p.at[1, chunk], target
            ).start()
            return carry

        lax.fori_loop(1, 32, body, 0)
        pltpu.make_async_copy(pout.at[chunk, :, pl.ds(16 * me, 16), :], place, sem_keep.at[2, chunk]).start()

    def arrive(chunk):
        bytes_of(xin.at[chunk, :, pl.ds(0, 448), :], sem_x.at[1, chunk])
        bytes_of(xin.at[chunk, :, pl.ds(0, 64), :], sem_keep.at[0, chunk])
        bytes_of(yin.at[chunk, pl.ds(0, 31)], sem_y.at[1, chunk])
        bytes_of(yin.at[chunk, 0], sem_keep.at[1, chunk])

    def gather(chunk):
        bytes_of(own.at[0, :, pl.ds(0, 31)], sem_p.at[1, chunk])
        bytes_of(own.at[0, :, 0], sem_keep.at[2, chunk])
        place = place_of(chunk)
        src = own.at[place]

        def to_partner(dst):
            remote(
                src, dst.at[place], sem_near.at[0, chunk], sem_near.at[1, chunk], across_rows(partner)
            ).start()

        @pl.when(is_kind(chunk, SHARED))
        def _():
            to_partner(own)

        @pl.when(jnp.logical_not(is_kind(chunk, SHARED)))
        def _():
            to_partner(nearby)

        @pl.when(is_inner)
        def _():
            remote(
                src, across.at[place], sem_across.at[0, chunk], sem_across.at[1, chunk], across_rows(other)
            ).start()

        @pl.when(is_outer & is_kind(chunk, SHARED))
        def _():
            remote(
                src, across.at[place], sem_far.at[0, chunk - 4], sem_far.at[1, chunk - 4], across_rows(far)
            ).start()

    def from_partner(chunk):
        bytes_of(own.at[0], sem_near.at[1, chunk])

    def from_other(chunk):
        bytes_of(own.at[0], sem_across.at[1, chunk])

    def turn(kind):
        def part(p, carry):
            def one(s, inside):
                square = jnp.concatenate([graw[kind, p, s], graw[kind, p, s + 16]], axis=0).astype(jnp.float32)
                swap[pl.ds(s, 128, stride=16), :] = square.T
                return inside

            lax.fori_loop(0, 16, one, 0)
            turned[kind, p] = swap[...].astype(jnp.bfloat16).reshape(32, 64, 128)
            return carry

        lax.fori_loop(0, 2, part, 0)

    lane = lax.broadcasted_iota(jnp.int32, (16, 128), 1)

    def correlate(chunk):
        for p in range(2):
            xcat[:, p * 128 : (p + 1) * 128] = xin[chunk, p]
        for p in range(2):
            for c in range(4):
                for k in range(4):
                    one = yin[chunk, c * 8 + 2 * k, p].astype(jnp.float32)
                    two = yin[chunk, c * 8 + 2 * k + 1, p].astype(jnp.float32)
                    first = jnp.where(lane < 64, one, pltpu.roll(two, 64, 1))
                    second = jnp.where(lane < 64, pltpu.roll(one, 64, 1), two)
                    base = p * 128 + c * 32
                    ycat[base : base + 16, k * 128 : (k + 1) * 128] = first.astype(jnp.bfloat16)
                    ycat[base + 16 : base + 32, k * 128 : (k + 1) * 128] = second.astype(jnp.bfloat16)
        spec_one[...] = jnp.dot(forward[...], xcat[...], preferred_element_type=jnp.float32)
        spec_two[...] = lax.dot_general(
            forward[...], ycat[...], (((1,), (1,)), ((), ())), preferred_element_type=jnp.float32
        )

        def mix(step, inner):
            cos_rows = pl.ds(step * 16, 16)
            sin_rows = pl.ds(FREQ + step * 16, 16)
            one_rr, one_ri = spec_one[cos_rows, 0:128], spec_one[cos_rows, 128:256]
            one_sr, one_si = spec_one[sin_rows, 0:128], spec_one[sin_rows, 128:256]
            two_rr, two_ri = spec_two[cos_rows, 0:128], spec_two[cos_rows, 128:256]
            two_sr, two_si = spec_two[sin_rows, 0:128], spec_two[sin_rows, 128:256]
            a_re, a_im = one_rr + one_si, one_ri - one_sr
            a_re_m, a_im_m = one_rr - one_si, one_ri + one_sr
            b_re, b_im = two_rr - two_si, two_ri + two_sr
            b_re_m, b_im_m = two_rr + two_si, two_ri - two_sr
            s_re = a_re * b_re - a_im * b_im
            s_im = a_re * b_im + a_im * b_re
            s_re_m = a_re_m * b_re_m - a_im_m * b_im_m
            s_im_m = a_re_m * b_im_m + a_im_m * b_re_m
            product[cos_rows, 0:128] = (s_re + s_re_m).astype(jnp.bfloat16)
            product[sin_rows, 0:128] = (s_im_m - s_im).astype(jnp.bfloat16)
            product[cos_rows, 128:256] = (s_im + s_im_m).astype(jnp.bfloat16)
            product[sin_rows, 128:256] = (s_re - s_re_m).astype(jnp.bfloat16)
            return inner

        lax.fori_loop(0, FREQ // 16, mix, 0)
        lagged = jnp.dot(inverse[...], product[...], preferred_element_type=jnp.float32)
        scale = 1.0 / (LENGTH * 32.0)
        pout[chunk, 0] = (scale * lagged[:, 128:256]).astype(jnp.bfloat16)
        pout[chunk, 1] = (-scale * lagged[:, 0:128]).astype(jnp.bfloat16)

    def apply_left(tiles, kind, side, column, parts=(0, 2)):
        def part(p, carry):
            swap[...] = tiles[pl.ds(4 * kind, 4), p].astype(jnp.float32).reshape(2048, 128)
            for pair in range(8):
                both = jnp.concatenate(
                    [
                        swap[pl.ds(2 * pair, 128, stride=16), :],
                        swap[pl.ds(2 * pair + 1, 128, stride=16), :],
                    ],
                    axis=1,
                ).astype(jnp.bfloat16)
                made = jnp.dot(left[side], both, preferred_element_type=jnp.float32)
                lower = pl.ds(256 * pair, 128)
                upper = pl.ds(256 * pair + 128, 128)
                total[p, column, lower, :] += made[:, 0:128]
                total[p, column, upper, :] += made[:, 128:256]
            return carry

        lax.fori_loop(*parts, part, 0)

    def finish_early(p, carry):
        def block(quad, inside):
            rows = pl.ds(quad * 512, 512)
            whole = jnp.concatenate([total[p, b, rows, :].astype(jnp.bfloat16) for b in range(5)], axis=1)
            for s in range(5):
                low, high = max(s - 1, 0) * 128, min(s + 2, 5) * 128
                made = jnp.dot(
                    whole[:, low:high],
                    right[low:high, s * 128 : s * 128 + 128],
                    preferred_element_type=jnp.float32,
                )
                for lag in range(4):
                    wide[p, s, pl.ds(quad * 4 + lag, 128, stride=16), :] = made[lag * 128 : lag * 128 + 128]
            return inside

        lax.fori_loop(0, 4, block, 0)
        for s in range(5):

            @pl.when((s < last - 1) | (s > last + 1))
            def _():
                staged[p, s] = wide[p, s].astype(jnp.bfloat16).reshape(128, 16, 128)
                pltpu.make_async_copy(staged.at[p, s], out.at[p, 0, s], sem_out.at[p, s]).start()

        return carry

    def finish_last(p, carry):
        swap[...] = nearby[pl.ds(8, 4), p].astype(jnp.float32).reshape(2048, 128)
        swap_two[...] = across[pl.ds(8, 4), p].astype(jnp.float32).reshape(2048, 128)
        both_left = jnp.concatenate([left[1 + toward], left[1 + inward]], axis=1)
        for pair in range(8):
            both = jnp.concatenate(
                [
                    jnp.concatenate(
                        [
                            held[pl.ds(2 * pair, 128, stride=16), :],
                            held[pl.ds(2 * pair + 1, 128, stride=16), :],
                        ],
                        axis=1,
                    )
                    for held in (swap, swap_two)
                ],
                axis=0,
            ).astype(jnp.bfloat16)
            made = jnp.dot(both_left, both, preferred_element_type=jnp.float32)
            lower = pl.ds(256 * pair, 128)
            upper = pl.ds(256 * pair + 128, 128)
            mixed[pl.ds(2 * pair, 128, stride=16), :] = made[:, 0:128] + total[p, last, lower, :]
            mixed[pl.ds(2 * pair + 1, 128, stride=16), :] = made[:, 128:256] + total[p, last, upper, :]
        for near in range(3):
            s = last + near - 1

            @pl.when((s >= 0) & (s < 5))
            def _():
                made = jnp.dot(
                    mixed[...].astype(jnp.bfloat16), right_last[near], preferred_element_type=jnp.float32
                )
                staged[p, s] = (wide[p, s] + made).astype(jnp.bfloat16).reshape(128, 16, 128)
                pltpu.make_async_copy(staged.at[p, s], out.at[p, 0, s], sem_out.at[p, s]).start()

        return carry

    send_x(jnp.int32(0))
    send_x(jnp.int32(1))
    load_diag.wait()
    turn(DIAG)
    send_y(jnp.int32(0))
    send_y(jnp.int32(1))

    @pl.when(is_outer)
    def _():
        bytes_of(graw.at[SHARED], sem_load.at[3])
        turn(SHARED)
        pltpu.make_async_copy(turned.at[SHARED, :, :, pl.ds(0, 32), :], ypass, sem_load.at[5]).start()
        remote(
            turned.at[SHARED, :, :, pl.ds(32, 32), :], ypass, sem_pass.at[2], sem_pass.at[3], across_rows(partner)
        ).start()

    place = lax.broadcasted_iota(jnp.int32, (128, 128), 1)
    orbital = lax.broadcasted_iota(jnp.int32, (128, 128), 0)
    order = (orbital == 4 * lax.rem(place, 32) + place // 32).astype(jnp.bfloat16)
    for side in range(3):
        left[side] = jnp.dot(coupling[row, side], order, preferred_element_type=jnp.float32).astype(jnp.bfloat16)
    for b in range(5):
        for s in range(max(b - 1, 0), min(b + 2, 5)):
            block = (slice(b * 128, b * 128 + 128), slice(s * 128, s * 128 + 128))
            tile_b, tile_c = row + b - 2, row + s - 2
            inside = (
                (tile_b >= 0) & (tile_b < 4) & (tile_c >= 0) & (tile_c < 4) & (b != last)
            ).astype(jnp.float32)
            safe = jnp.clip(tile_c, 0, 3)
            tile = coupling[safe, b - s + 1].astype(jnp.float32) * inside
            right[block] = tile.T.astype(jnp.bfloat16)

    for near in range(3):
        tile_b, tile_c = row + last - 2, row + last - 2 + near - 1
        inside = ((tile_c >= 0) & (tile_c < 4)).astype(jnp.float32)
        tile = coupling[jnp.clip(tile_c, 0, 3), 2 - near].astype(jnp.float32) * inside
        right_last[near] = tile.T.astype(jnp.bfloat16)

    @pl.when(is_outer)
    def _():
        for place in range(8, 12):
            across[place] = jnp.zeros((2, 32, 16, 128), jnp.bfloat16)

    def clear(step, carry):
        for b in range(5):
            total[0, b, pl.ds(step * 256, 256), :] = jnp.zeros((256, 128), jnp.float32)
            total[1, b, pl.ds(step * 256, 256), :] = jnp.zeros((256, 128), jnp.float32)
        return carry

    lax.fori_loop(0, 8, clear, 0)
    load_forward.wait()
    load_inverse.wait()


    def step(chunk, carry):
        arrive(chunk)
        correlate(chunk)
        send_p(chunk)
        ahead = chunk + AHEAD

        @pl.when(ahead == 4)
        def _():
            @pl.when(is_outer)
            def _():
                bytes_of(xpass, sem_pass.at[1])
                bytes_of(ypass, sem_load.at[5])

            @pl.when(is_inner)
            def _():
                bytes_of(xpass, sem_load.at[4])
                bytes_of(ypass, sem_pass.at[3])

        @pl.when(ahead == 6)
        def _():
            bytes_of(graw.at[INWARD], sem_raw.at[2])
            turn(INWARD)

        @pl.when(ahead < CHUNKS)
        def _():
            send_x(ahead)
            send_y(ahead)

        @pl.when(chunk >= 1)
        def _():
            gather(chunk - 1)

        @pl.when(chunk == 6)
        def _():
            apply_left(own, 0, 1, 2)

        @pl.when(chunk == 9)
        def _():
            for early in range(4):
                from_partner(early)
            apply_left(nearby, 0, 1 + toward, 2 + toward)

        return carry

    lax.fori_loop(0, CHUNKS, step, 0)

    @pl.when(is_inner)
    def _():
        for early in range(4):
            from_other(early)
        apply_left(across, 0, 1 + inward, 2 + inward)

    gather(jnp.int32(9))
    from_partner(4)
    from_partner(5)
    apply_left(own, 1, 1 + inward * (1 - inner), 2 - inward * inner)
    apply_left(own, 2, 1, 2 + inward)

    @pl.when(is_inner)
    def _():
        for chunk in range(4, 6):
            from_other(chunk)
            bytes_of(own.at[0], sem_far.at[1, chunk - 4])
        apply_left(across, 1, 1 + inward, 2 + 2 * inward)

    lax.fori_loop(0, 2, finish_early, 0)
    for chunk in range(6, CHUNKS):
        from_partner(chunk)

    @pl.when(is_inner)
    def _():
        for chunk in range(6, CHUNKS):
            from_other(chunk)

    lax.fori_loop(0, 2, finish_last, 0)
    for p in range(2):
        for s in range(5):
            pltpu.make_async_copy(staged.at[p, s], out.at[p, 0, s], sem_out.at[p, s]).wait()

    @pl.when(is_inner)
    def _():
        bytes_of(xpass, sem_pass.at[0])
        bytes_of(graw.at[INWARD], sem_raw.at[0])
        bytes_of(graw.at[INWARD], sem_raw.at[1])

    @pl.when(is_outer)
    def _():
        bytes_of(ypass, sem_pass.at[2])
        for chunk in range(4, 6):
            bytes_of(own.at[0], sem_far.at[0, chunk - 4])

    def sent(chunk, carry):
        bytes_of(xin.at[chunk, :, pl.ds(0, 448), :], sem_x.at[0, chunk])
        bytes_of(yin.at[chunk, pl.ds(0, 31)], sem_y.at[0, chunk])
        bytes_of(own.at[0, :, pl.ds(0, 31)], sem_p.at[0, chunk])
        bytes_of(own.at[0], sem_near.at[0, chunk])

        @pl.when(is_inner)
        def _():
            bytes_of(own.at[0], sem_across.at[0, chunk])

        return carry

    lax.fori_loop(0, CHUNKS, sent, 0)


def shards(lesser, greater, coupling):
    forward, inverse = tables(512)
    half = jnp.bfloat16
    whole = jnp.float32
    anywhere = pl.BlockSpec(memory_space=pl.ANY)
    return pl.pallas_call(
        kernel,
        out_shape=jax.ShapeDtypeStruct((2, 1, 5, 128, 16, 128), half),
        in_specs=[anywhere, anywhere, pl.BlockSpec(memory_space=pltpu.VMEM), anywhere, anywhere],
        out_specs=anywhere,
        scratch_shapes=[
            pltpu.VMEM((LENGTH, 512), half),
            pltpu.VMEM((512, LENGTH), half),
            pltpu.VMEM((3, 2, 32, 64, 128), half),
            pltpu.VMEM((3, 2, 32, 64, 128), half),
            pltpu.VMEM((2, 8, 2, 64, 128), half),
            pltpu.VMEM((2, 32, 32, 128), half),
            pltpu.VMEM((CHUNKS, 2, 512, 128), half),
            pltpu.VMEM((CHUNKS, 32, 2, 16, 128), half),
            pltpu.VMEM((CHUNKS, 2, 512, 128), half),
            pltpu.VMEM((12, 2, 32, 16, 128), half),
            pltpu.VMEM((12, 2, 32, 16, 128), half),
            pltpu.VMEM((12, 2, 32, 16, 128), half),
            pltpu.VMEM((2, 5, 2048, 128), whole),
            pltpu.VMEM((2048, 128), whole),
            pltpu.VMEM((2048, 128), whole),
            pltpu.VMEM((2048, 128), whole),
            pltpu.VMEM((2, 5, 2048, 128), whole),
            pltpu.VMEM((3, 128, 128), half),
            pltpu.VMEM((640, 640), half),
            pltpu.VMEM((3, 128, 128), half),
            pltpu.VMEM((512, 256), half),
            pltpu.VMEM((256, 512), half),
            pltpu.VMEM((LENGTH, 256), whole),
            pltpu.VMEM((LENGTH, 256), whole),
            pltpu.VMEM((LENGTH, 256), half),
            pltpu.VMEM((2, 5, 128, 16, 128), half),
            pltpu.SemaphoreType.DMA((6,)),
            pltpu.SemaphoreType.DMA((3, CHUNKS)),
            pltpu.SemaphoreType.DMA((3,)),
            pltpu.SemaphoreType.DMA((4,)),
            pltpu.SemaphoreType.DMA((2, CHUNKS)),
            pltpu.SemaphoreType.DMA((2, CHUNKS)),
            pltpu.SemaphoreType.DMA((2, CHUNKS)),
            pltpu.SemaphoreType.DMA((2, CHUNKS)),
            pltpu.SemaphoreType.DMA((2, CHUNKS)),
            pltpu.SemaphoreType.DMA((2, 2)),
            pltpu.SemaphoreType.DMA((2, 5)),
        ],
        compiler_params=pltpu.CompilerParams(
            collective_id=0, has_side_effects=True, vmem_limit_bytes=60 * 1024 * 1024
        ),
        cost_estimate=pl.CostEstimate(flops=10**10, bytes_accessed=2 * 10**7, transcendentals=0),
    )(
        lesser.reshape(2, 3, 8, 4, 64, 128),
        greater.reshape(2, 3, 32, 64, 128),
        coupling,
        jnp.asarray(forward),
        jnp.asarray(inverse),
    )


def solution(mesh):
    placed = (P(None, "row", None, "col", "en", None), P(None, "row", None, "col", "en", None), P())
    return jax.shard_map(
        shards,
        mesh=mesh,
        in_specs=placed,
        out_specs=P(None, "row", None, None, ("col", "en"), None),
        check_vma=False,
    )
```

time: 144 us -> 125 us (0.87)
  Pallas kernels: 137 us -> 119 us
    pallas_call x1, Pallas kernels: 137 us -> 119 us  [shards(): pl.pallas_call(kernel, out_shape=jax.ShapeDtypeStruct((2, 1, 5, 128, 16,...]
where the time goes in v3:
time: 125 us
  Pallas kernels  119 us (95%)
  local copies, waits for them, and re-layouts  5.79 us (5%)
    pallas_call x1, Pallas kernels, shards(): pl.pallas_call(kernel, out_shape=jax.ShapeDtypeStruct((2, 1, 5, 128, 16,...  119 us
    unnamed x1, local copies, waits for them, and re-layouts  5.79 us

profile of v3, /device:TPU:9, one launch (start us, length us, event | category | flops | bytes accessed | tf_op | source)
XLA Modules:
  0.0 125.3 jit_solution(18404877140148482439)
XLA Ops:
  0.0 119.5 %shard_map.55 = bf16[2,1,5,128,16,128]{5,4,3,2,1,0:T(8,128)(2,1)} custom-call(bf16[2,3,8,4,64,128]{5,4,3,2,1,0:T(8,128)(2,1)} %bitcast.2, bf16[2,3,32,64,128]{4,3,2,1,0:T(8,128)(2,1)} %bitcast.3, bf16[4,3,128,128]{3,2,1,0:T(8,128)(2,1)} %coupling.1, bf16[768,512]{1,0:T(8,128)(2,1)} %constant.4.clone.forward_hbm, bf16[512,768]{1,0:T(8,128)(2,1)} %constant.5.clone.inverse_hbm), custom_call_target="tpu_custom_call" | custom-call | flops 10000000000 | bytes 20000000 | tf_op jit(solution)/shard_map/pallas_call | solution.py:569
  119.5 5.8 %copy.7 = bf16[2,1,5,128,16,128]{5,4,3,2,1,0:T(8,128)(2,1)} copy(bf16[2,1,5,128,16,128]{5,4,3,2,1,0:T(8,128)(2,1)} %shard_map.55) | data formatting | bytes 10485760

commit v4 on v3

--- a/solution.py
+++ b/solution.py
@@ -62,7 +62,6 @@
     spec_one,
     spec_two,
     product,
-    staged,
     sem_load,
     sem_keep,
     sem_raw,
@@ -73,7 +72,6 @@
     sem_near,
     sem_across,
     sem_far,
-    sem_out,
 ):
     row = lax.axis_index("row")
     col = lax.axis_index("col")
@@ -360,8 +358,7 @@
 
             @pl.when((s < last - 1) | (s > last + 1))
             def _():
-                staged[p, s] = wide[p, s].astype(jnp.bfloat16).reshape(128, 16, 128)
-                pltpu.make_async_copy(staged.at[p, s], out.at[p, 0, s], sem_out.at[p, s]).start()
+                out[p, 0, s] = wide[p, s].astype(jnp.bfloat16).reshape(128, 16, 128)
 
         return carry
 
@@ -396,8 +393,7 @@
                 made = jnp.dot(
                     mixed[...].astype(jnp.bfloat16), right_last[near], preferred_element_type=jnp.float32
                 )
-                staged[p, s] = (wide[p, s] + made).astype(jnp.bfloat16).reshape(128, 16, 128)
-                pltpu.make_async_copy(staged.at[p, s], out.at[p, 0, s], sem_out.at[p, s]).start()
+                out[p, 0, s] = (wide[p, s] + made).astype(jnp.bfloat16).reshape(128, 16, 128)
 
         return carry
 
@@ -530,10 +526,6 @@
             from_other(chunk)
 
     lax.fori_loop(0, 2, finish_last, 0)
-    for p in range(2):
-        for s in range(5):
-            pltpu.make_async_copy(staged.at[p, s], out.at[p, 0, s], sem_out.at[p, s]).wait()
-
     @pl.when(is_inner)
     def _():
         bytes_of(xpass, sem_pass.at[0])
@@ -568,9 +560,9 @@
     anywhere = pl.BlockSpec(memory_space=pl.ANY)
     return pl.pallas_call(
         kernel,
-        out_shape=jax.ShapeDtypeStruct((2, 1, 5, 128, 16, 128), half),
+        out_shape=pltpu.VMEM((2, 1, 5, 128, 16, 128), half),
         in_specs=[anywhere, anywhere, pl.BlockSpec(memory_space=pltpu.VMEM), anywhere, anywhere],
-        out_specs=anywhere,
+        out_specs=pl.BlockSpec(memory_space=pltpu.VMEM),
         scratch_shapes=[
             pltpu.VMEM((LENGTH, 512), half),
             pltpu.VMEM((512, LENGTH), half),
@@ -597,7 +589,6 @@
             pltpu.VMEM((LENGTH, 256), whole),
             pltpu.VMEM((LENGTH, 256), whole),
             pltpu.VMEM((LENGTH, 256), half),
-            pltpu.VMEM((2, 5, 128, 16, 128), half),
             pltpu.SemaphoreType.DMA((6,)),
             pltpu.SemaphoreType.DMA((3, CHUNKS)),
             pltpu.SemaphoreType.DMA((3,)),
@@ -608,10 +599,9 @@
             pltpu.SemaphoreType.DMA((2, CHUNKS)),
             pltpu.SemaphoreType.DMA((2, CHUNKS)),
             pltpu.SemaphoreType.DMA((2, 2)),
-            pltpu.SemaphoreType.DMA((2, 5)),
         ],
         compiler_params=pltpu.CompilerParams(
-            collective_id=0, has_side_effects=True, vmem_limit_bytes=60 * 1024 * 1024
+            collective_id=0, has_side_effects=True, vmem_limit_bytes=55 * 1024 * 1024
         ),
         cost_estimate=pl.CostEstimate(flops=10**10, bytes_accessed=2 * 10**7, transcendentals=0),
     )(

time: 125 us -> 121 us (0.968)
  local copies, waits for them, and re-layouts: 5.79 us -> 2.36 us
    unnamed x1, local copies, waits for them, and re-layouts: 5.79 us -> 2.36 us
where the time goes in v4:
time: 121 us
  Pallas kernels  119 us (98%)
  local copies, waits for them, and re-layouts  2.36 us (2%)
    pallas_call x1, Pallas kernels, shards(): pl.pallas_call(kernel, out_shape=pltpu.VMEM((2, 1, 5, 128, 16, 128), half...  119 us

profile of v4, /device:TPU:9, one launch (start us, length us, event | category | flops | bytes accessed | tf_op | source)
XLA Modules:
  0.0 121.0 jit_solution(16911305805217340927)
XLA Ops:
  0.0 118.6 %shard_map.55 = bf16[2,1,5,128,16,128]{5,4,3,2,1,0:T(8,128)(2,1)S(1)} custom-call(bf16[2,3,8,4,64,128]{5,4,3,2,1,0:T(8,128)(2,1)} %bitcast.2, bf16[2,3,32,64,128]{4,3,2,1,0:T(8,128)(2,1)} %bitcast.3, bf16[4,3,128,128]{3,2,1,0:T(8,128)(2,1)} %coupling.1, bf16[768,512]{1,0:T(8,128)(2,1)} %constant.4.clone.forward_hbm, bf16[512,768]{1,0:T(8,128)(2,1)} %constant.5.clone.inverse_hbm), custom_call_target="tpu_custom_call" | custom-call | flops 10000000000 | bytes 20000000 | tf_op jit(solution)/shard_map/pallas_call | solution.py:561
  118.6 2.4 %copy.7 = bf16[2,1,5,128,16,128]{5,4,3,2,1,0:T(8,128)(2,1)} copy(bf16[2,1,5,128,16,128]{5,4,3,2,1,0:T(8,128)(2,1)S(1)} %shard_map.55) | data formatting | bytes 10485760

commit v5 on v4

--- a/solution.py
+++ b/solution.py
@@ -252,6 +252,30 @@
                 src, across.at[place], sem_far.at[0, chunk - 4], sem_far.at[1, chunk - 4], across_rows(far)
             ).start()
 
+    def gather_last():
+        chunk = CHUNKS - 1
+        bytes_of(own.at[0, :, pl.ds(0, 31)], sem_p.at[1, chunk])
+        bytes_of(own.at[0, :, 0], sem_keep.at[2, chunk])
+        place = chunk + 2
+        for p in range(2):
+            remote(
+                own.at[place, p],
+                nearby.at[place, p],
+                sem_near.at[0, chunk + p],
+                sem_near.at[1, chunk + p],
+                across_rows(partner),
+            ).start()
+
+            @pl.when(is_inner)
+            def _():
+                remote(
+                    own.at[place, p],
+                    across.at[place, p],
+                    sem_across.at[0, chunk + p],
+                    sem_across.at[1, chunk + p],
+                    across_rows(other),
+                ).start()
+
     def from_partner(chunk):
         bytes_of(own.at[0], sem_near.at[1, chunk])
 
@@ -312,7 +336,7 @@
             product[sin_rows, 128:256] = (s_re - s_re_m).astype(jnp.bfloat16)
             return inner
 
-        lax.fori_loop(0, FREQ // 16, mix, 0)
+        lax.fori_loop(0, FREQ // 16, mix, 0, unroll=4)
         lagged = jnp.dot(inverse[...], product[...], preferred_element_type=jnp.float32)
         scale = 1.0 / (LENGTH * 32.0)
         pout[chunk, 0] = (scale * lagged[:, 128:256]).astype(jnp.bfloat16)
@@ -342,15 +366,17 @@
         def block(quad, inside):
             rows = pl.ds(quad * 512, 512)
             whole = jnp.concatenate([total[p, b, rows, :].astype(jnp.bfloat16) for b in range(5)], axis=1)
-            for s in range(5):
-                low, high = max(s - 1, 0) * 128, min(s + 2, 5) * 128
+            for first, count, low, high in ((0, 2, 0, 384), (2, 2, 128, 640), (4, 1, 384, 640)):
                 made = jnp.dot(
                     whole[:, low:high],
-                    right[low:high, s * 128 : s * 128 + 128],
+                    right[low:high, first * 128 : (first + count) * 128],
                     preferred_element_type=jnp.float32,
                 )
-                for lag in range(4):
-                    wide[p, s, pl.ds(quad * 4 + lag, 128, stride=16), :] = made[lag * 128 : lag * 128 + 128]
+                for s in range(first, first + count):
+                    for lag in range(4):
+                        wide[p, s, pl.ds(quad * 4 + lag, 128, stride=16), :] = made[
+                            lag * 128 : lag * 128 + 128, (s - first) * 128 : (s - first) * 128 + 128
+                        ]
             return inside
 
         lax.fori_loop(0, 4, block, 0)
@@ -363,6 +389,12 @@
         return carry
 
     def finish_last(p, carry):
+        bytes_of(own.at[0, 0], sem_near.at[1, CHUNKS - 1 + p])
+
+        @pl.when(is_inner)
+        def _():
+            bytes_of(own.at[0, 0], sem_across.at[1, CHUNKS - 1 + p])
+
         swap[...] = nearby[pl.ds(8, 4), p].astype(jnp.float32).reshape(2048, 128)
         swap_two[...] = across[pl.ds(8, 4), p].astype(jnp.float32).reshape(2048, 128)
         both_left = jnp.concatenate([left[1 + toward], left[1 + inward]], axis=1)
@@ -418,6 +450,8 @@
     order = (orbital == 4 * lax.rem(place, 32) + place // 32).astype(jnp.bfloat16)
     for side in range(3):
         left[side] = jnp.dot(coupling[row, side], order, preferred_element_type=jnp.float32).astype(jnp.bfloat16)
+    for b, s in ((2, 0), (1, 3), (4, 2)):
+        right[b * 128 : b * 128 + 128, s * 128 : s * 128 + 128] = jnp.zeros((128, 128), jnp.bfloat16)
     for b in range(5):
         for s in range(max(b - 1, 0), min(b + 2, 5)):
             block = (slice(b * 128, b * 128 + 128), slice(s * 128, s * 128 + 128))
@@ -453,9 +487,18 @@
 
     def step(chunk, carry):
         arrive(chunk)
+        ahead = chunk + AHEAD
+
+        @pl.when(ahead < 4)
+        def _():
+            send_x(ahead)
+
+        @pl.when((ahead > 6) & (ahead < CHUNKS))
+        def _():
+            send_x(ahead)
+
         correlate(chunk)
         send_p(chunk)
-        ahead = chunk + AHEAD
 
         @pl.when(ahead == 4)
         def _():
@@ -476,7 +519,10 @@
 
         @pl.when(ahead < CHUNKS)
         def _():
-            send_x(ahead)
+            @pl.when((ahead >= 4) & (ahead <= 6))
+            def _():
+                send_x(ahead)
+
             send_y(ahead)
 
         @pl.when(chunk >= 1)
@@ -487,26 +533,26 @@
         def _():
             apply_left(own, 0, 1, 2)
 
-        @pl.when(chunk == 9)
+        @pl.when(chunk == 7)
         def _():
             for early in range(4):
                 from_partner(early)
             apply_left(nearby, 0, 1 + toward, 2 + toward)
 
+        @pl.when((chunk == 8) & is_inner)
+        def _():
+            for early in range(4):
+                from_other(early)
+            apply_left(across, 0, 1 + inward, 2 + inward)
+
         return carry
 
     lax.fori_loop(0, CHUNKS, step, 0)
 
-    @pl.when(is_inner)
-    def _():
-        for early in range(4):
-            from_other(early)
-        apply_left(across, 0, 1 + inward, 2 + inward)
-
-    gather(jnp.int32(9))
     from_partner(4)
     from_partner(5)
     apply_left(own, 1, 1 + inward * (1 - inner), 2 - inward * inner)
+    gather_last()
     apply_left(own, 2, 1, 2 + inward)
 
     @pl.when(is_inner)
@@ -517,12 +563,12 @@
         apply_left(across, 1, 1 + inward, 2 + 2 * inward)
 
     lax.fori_loop(0, 2, finish_early, 0)
-    for chunk in range(6, CHUNKS):
+    for chunk in range(6, CHUNKS - 1):
         from_partner(chunk)
 
     @pl.when(is_inner)
     def _():
-        for chunk in range(6, CHUNKS):
+        for chunk in range(6, CHUNKS - 1):
             from_other(chunk)
 
     lax.fori_loop(0, 2, finish_last, 0)
@@ -542,6 +588,9 @@
         bytes_of(xin.at[chunk, :, pl.ds(0, 448), :], sem_x.at[0, chunk])
         bytes_of(yin.at[chunk, pl.ds(0, 31)], sem_y.at[0, chunk])
         bytes_of(own.at[0, :, pl.ds(0, 31)], sem_p.at[0, chunk])
+        return carry
+
+    def passed_on(chunk, carry):
         bytes_of(own.at[0], sem_near.at[0, chunk])
 
         @pl.when(is_inner)
@@ -551,6 +600,13 @@
         return carry
 
     lax.fori_loop(0, CHUNKS, sent, 0)
+    lax.fori_loop(0, CHUNKS - 1, passed_on, 0)
+    for p in range(2):
+        bytes_of(own.at[0, 0], sem_near.at[0, CHUNKS - 1 + p])
+
+        @pl.when(is_inner)
+        def _():
+            bytes_of(own.at[0, 0], sem_across.at[0, CHUNKS - 1 + p])
 
 
 def shards(lesser, greater, coupling):
@@ -596,8 +652,8 @@
             pltpu.SemaphoreType.DMA((2, CHUNKS)),
             pltpu.SemaphoreType.DMA((2, CHUNKS)),
             pltpu.SemaphoreType.DMA((2, CHUNKS)),
-            pltpu.SemaphoreType.DMA((2, CHUNKS)),
-            pltpu.SemaphoreType.DMA((2, CHUNKS)),
+            pltpu.SemaphoreType.DMA((2, CHUNKS + 1)),
+            pltpu.SemaphoreType.DMA((2, CHUNKS + 1)),
             pltpu.SemaphoreType.DMA((2, 2)),
         ],
         compiler_params=pltpu.CompilerParams(

time: 121 us -> 118 us (0.975)
  Pallas kernels: 119 us -> 115 us
    pallas_call x1, Pallas kernels: 119 us -> 115 us  [shards(): pl.pallas_call(kernel, out_shape=pltpu.VMEM((2, 1, 5, 128, 16, 128), half...]
where the time goes in v5:
time: 118 us
  Pallas kernels  115 us (97%)
  local copies, waits for them, and re-layouts  2.36 us (2%)
    pallas_call x1, Pallas kernels, shards(): pl.pallas_call(kernel, out_shape=pltpu.VMEM((2, 1, 5, 128, 16, 128), half...  115 us
    unnamed x1, local copies, waits for them, and re-layouts  2.36 us

profile of v5, /device:TPU:9, one launch (start us, length us, event | category | flops | bytes accessed | tf_op | source)
XLA Modules:
  0.0 117.6 jit_solution(6464281384238896215)
XLA Ops:
  0.0 115.2 %shard_map.55 = bf16[2,1,5,128,16,128]{5,4,3,2,1,0:T(8,128)(2,1)S(1)} custom-call(bf16[2,3,8,4,64,128]{5,4,3,2,1,0:T(8,128)(2,1)} %bitcast.2, bf16[2,3,32,64,128]{4,3,2,1,0:T(8,128)(2,1)} %bitcast.3, bf16[4,3,128,128]{3,2,1,0:T(8,128)(2,1)} %coupling.1, bf16[768,512]{1,0:T(8,128)(2,1)} %constant.4.clone.forward_hbm, bf16[512,768]{1,0:T(8,128)(2,1)} %constant.5.clone.inverse_hbm), custom_call_target="tpu_custom_call" | custom-call | flops 10000000000 | bytes 20000000 | tf_op jit(solution)/shard_map/pallas_call | solution.py:617
  115.2 2.4 %copy.7 = bf16[2,1,5,128,16,128]{5,4,3,2,1,0:T(8,128)(2,1)} copy(bf16[2,1,5,128,16,128]{5,4,3,2,1,0:T(8,128)(2,1)S(1)} %shard_map.55) | data formatting | bytes 10485760

commit v6 on v5

--- a/solution.py
+++ b/solution.py
@@ -289,7 +289,7 @@
                 swap[pl.ds(s, 128, stride=16), :] = square.T
                 return inside
 
-            lax.fori_loop(0, 16, one, 0)
+            lax.fori_loop(0, 16, one, 0, unroll=4)
             turned[kind, p] = swap[...].astype(jnp.bfloat16).reshape(32, 64, 128)
             return carry
 
@@ -336,7 +336,7 @@
             product[sin_rows, 128:256] = (s_re - s_re_m).astype(jnp.bfloat16)
             return inner
 
-        lax.fori_loop(0, FREQ // 16, mix, 0, unroll=4)
+        lax.fori_loop(0, FREQ // 16, mix, 0, unroll=8)
         lagged = jnp.dot(inverse[...], product[...], preferred_element_type=jnp.float32)
         scale = 1.0 / (LENGTH * 32.0)
         pout[chunk, 0] = (scale * lagged[:, 128:256]).astype(jnp.bfloat16)

time: 118 us -> 118 us (level)
  no operation moved by 1% of the time
where the time goes in v6:
time: 118 us
  Pallas kernels  115 us (97%)
  local copies, waits for them, and re-layouts  2.36 us (2%)
    pallas_call x1, Pallas kernels, shards(): pl.pallas_call(kernel, out_shape=pltpu.VMEM((2, 1, 5, 128, 16, 128), half...  115 us
    unnamed x1, local copies, waits for them, and re-layouts  2.36 us

profile of v6, /device:TPU:9, one launch (start us, length us, event | category | flops | bytes accessed | tf_op | source)
XLA Modules:
  0.0 117.6 jit_solution(9268502899516774854)
XLA Ops:
  0.0 115.3 %shard_map.55 = bf16[2,1,5,128,16,128]{5,4,3,2,1,0:T(8,128)(2,1)S(1)} custom-call(bf16[2,3,8,4,64,128]{5,4,3,2,1,0:T(8,128)(2,1)} %bitcast.2, bf16[2,3,32,64,128]{4,3,2,1,0:T(8,128)(2,1)} %bitcast.3, bf16[4,3,128,128]{3,2,1,0:T(8,128)(2,1)} %coupling.1, bf16[768,512]{1,0:T(8,128)(2,1)} %constant.4.clone.forward_hbm, bf16[512,768]{1,0:T(8,128)(2,1)} %constant.5.clone.inverse_hbm), custom_call_target="tpu_custom_call" | custom-call | flops 10000000000 | bytes 20000000 | tf_op jit(solution)/shard_map/pallas_call | solution.py:617
  115.3 2.4 %copy.7 = bf16[2,1,5,128,16,128]{5,4,3,2,1,0:T(8,128)(2,1)} copy(bf16[2,1,5,128,16,128]{5,4,3,2,1,0:T(8,128)(2,1)S(1)} %shard_map.55) | data formatting | bytes 10485760
